TPU v7x, 32 devices: a whole 2x2x4 slice. The times are simulated.
32 devices in a mesh: blk: 4 (over z), head: 4 (over x, core), fsdp: 2 (over y).
Axes of the slice: x: 2, y: 2, z: 4, core: 2. Of those that a mesh axis runs over, the one named last changes fastest.
Arguments:
- tokens: bfloat16 [2, 4096, 1536], P('fsdp', ('blk', 'head')), may hold values from -6 to 6
- documents: int32 [2, 4096], P('fsdp'), may hold values from 0 to 3, as said below
- routes: int32 [2, 4096, 4], P('fsdp', ('blk', 'head')), may hold values from 0 to 7, all different within a row; in each aligned block of 256 rows (0 to 255, 256 to 511, ..., all dimensions but the last counted through in order) at most 192 rows name the same one
- cotangent: bfloat16 [2, 4096, 1536], P('fsdp', ('blk', 'head')), may hold values from -6 to 6
- first_gain: bfloat16 [1536], P('fsdp'), may hold values from 0.5 to 1.5
- query_weight: bfloat16 [1536, 1536], P('fsdp'), may hold values from -0.15625 to 0.15625
- keyvalue_weight: bfloat16 [1536, 512], P('fsdp'), may hold values from -0.15625 to 0.15625
- output_weight: bfloat16 [1536, 1536], P('fsdp'), may hold values from -3 to 3
- second_gain: bfloat16 [1536], P('fsdp'), may hold values from 0.5 to 1.5
- router_weight: bfloat16 [1536, 8], P('fsdp'), may hold values from -0.078125 to 0.078125
- expert_in: bfloat16 [8, 1536, 1536], P('blk', 'fsdp'), may hold values from -0.15625 to 0.15625
- expert_out: bfloat16 [8, 768, 1536], P('blk', None, 'fsdp'), may hold values from -0.625 to 0.625
Outputs:
- block_out: bfloat16 [2, 4096, 1536], P('fsdp', ('blk', 'head'))
- tokens_grad: bfloat16 [2, 4096, 1536], P('fsdp', ('blk', 'head'))
- first_gain_grad: float32 [1536], P('fsdp')
- query_grad: float32 [1536, 1536], P('fsdp')
- keyval_grad: float32 [1536, 512], P('fsdp')
- output_grad: float32 [1536, 1536], P('fsdp')
- second_gain_grad: float32 [1536], P('fsdp')
- router_grad: float32 [1536, 8], P('fsdp')
- expert_in_grad: float32 [8, 1536, 1536], P('blk', 'fsdp')
- expert_out_grad: float32 [8, 768, 1536], P('blk', None, 'fsdp')
Inputs may be any that keep to these rules, and one draw needn't show every extreme that they name: `documents`: document numbers never fall along a sequence. `routes`: A token names 4 different experts; within the 256 rows of one device of a sequence no expert is named more than 192 times.
All inputs are finite; a program needn't handle non-finite values.
Results may differ from a plain program's by a relative error of at most 0.025.
Values may be sent and summed in bfloat16 or wider, within the bound.
A program may use at most 256 MiB of HBM per device.

v0:
```python
import jax
import jax.numpy as jnp
from jax import lax
from jax.sharding import PartitionSpec as P

QUERY_HEADS = 12
KEYVALUE_HEADS = 2
HEAD_SIZE = 128
TOP = 4


NORM_EPSILON = 1e-06
ROPE_BASE = 1000000.0
MASKED_SCORE = -1e30
EXACT = lax.Precision.HIGHEST


def rms_scale(value_tensor, gain):
    return (
        value_tensor
        * lax.rsqrt(jnp.mean(value_tensor * value_tensor, axis=-1, keepdims=True) + NORM_EPSILON)
        * gain
    )


def apply_rotary(value_tensor, token_positions, direction):
    half_dim = value_tensor.shape[-1] // 2
    inverse = jnp.power(
        ROPE_BASE, -jnp.arange(half_dim).astype(jnp.float32) * 2.0 / value_tensor.shape[-1]
    )
    angle = token_positions[:, None] * inverse[None, :]
    cosine = jnp.cos(angle)[:, None, :]
    sine = direction * jnp.sin(angle)[:, None, :]
    first_half = value_tensor[..., :half_dim]
    second_half = value_tensor[..., half_dim:]
    return jnp.concatenate(
        [first_half * cosine - second_half * sine, second_half * cosine + first_half * sine],
        axis=-1,
    )


def gated_unit(gate_up):
    half_width = gate_up.shape[-1] // 2
    return jax.nn.gelu(gate_up[..., :half_width], approximate=True) * gate_up[..., half_width:]


def on_device(
    tokens,
    documents,
    routes,
    cotangent,
    first_gain,
    query_weight,
    keyvalue_weight,
    output_weight,
    second_gain,
    router_weight,
    expert_in,
    expert_out,
):
    gain_one, weight_q, weight_kv, weight_o, gain_two, weight_r, weight_in, weight_out = (
        lax.all_gather(first_gain, "fsdp", axis=0, tiled=True),
        lax.all_gather(query_weight, "fsdp", axis=0, tiled=True),
        lax.all_gather(keyvalue_weight, "fsdp", axis=0, tiled=True),
        lax.all_gather(output_weight, "fsdp", axis=0, tiled=True),
        lax.all_gather(second_gain, "fsdp", axis=0, tiled=True),
        lax.all_gather(router_weight, "fsdp", axis=0, tiled=True),
        lax.all_gather(expert_in, "fsdp", axis=1, tiled=True),
        lax.all_gather(expert_out, "fsdp", axis=2, tiled=True),
    )
    head_count = lax.axis_size("head")
    block_count = lax.axis_size("blk")
    head_index = lax.axis_index("head")
    block_index = lax.axis_index("blk")
    sequence_rows = tokens.shape[1]
    model_width = tokens.shape[2]
    group_rows = head_count * sequence_rows
    sequence_length = block_count * group_rows
    local_heads = QUERY_HEADS // head_count
    queries_per_keyvalue = QUERY_HEADS // KEYVALUE_HEADS
    keyvalue_width = 2 * KEYVALUE_HEADS * HEAD_SIZE
    expert_count = weight_r.shape[1]
    local_experts = weight_in.shape[0]
    capacity = 3 * sequence_rows * TOP // (2 * expert_count)
    score_scale = HEAD_SIZE ** (-0.5)
    x_float = tokens[0].astype(jnp.float32)
    row_start = (block_index * head_count + head_index) * sequence_rows
    token_positions = (row_start + jnp.arange(sequence_rows, dtype=jnp.int32)).astype(jnp.float32)
    normed_one = rms_scale(x_float, gain_one).astype(jnp.bfloat16)
    query_pre = jnp.dot(normed_one, weight_q, preferred_element_type=jnp.float32)
    prerotation_keyvalue = jnp.dot(normed_one, weight_kv, preferred_element_type=jnp.float32)
    query_rot = apply_rotary(
        query_pre.reshape(sequence_rows, QUERY_HEADS, HEAD_SIZE), token_positions, 1.0
    ).astype(jnp.bfloat16)
    rotated_keys = apply_rotary(
        prerotation_keyvalue[:, : KEYVALUE_HEADS * HEAD_SIZE].reshape(
            sequence_rows, KEYVALUE_HEADS, HEAD_SIZE
        ),
        token_positions,
        1.0,
    )
    keyval_rows = jnp.concatenate(
        [
            rotated_keys.reshape(sequence_rows, KEYVALUE_HEADS * HEAD_SIZE),
            prerotation_keyvalue[:, KEYVALUE_HEADS * HEAD_SIZE :],
        ],
        axis=1,
    ).astype(jnp.bfloat16)
    query_in, keyval_in = (
        lax.all_to_all(
            query_rot.reshape(sequence_rows, head_count, local_heads * HEAD_SIZE),
            "head",
            split_axis=1,
            concat_axis=0,
            tiled=True,
        ),
        lax.all_to_all(
            jnp.broadcast_to(keyval_rows[:, None, :], (sequence_rows, head_count, keyvalue_width)),
            "head",
            split_axis=1,
            concat_axis=0,
            tiled=True,
        ),
    )
    query_group = query_in.reshape(group_rows, local_heads, HEAD_SIZE)
    keyval_group = keyval_in.reshape(group_rows, keyvalue_width)
    head_of = (
        head_index * local_heads + jnp.arange(local_heads, dtype=jnp.int32)
    ) // queries_per_keyvalue
    slotted_heads = jnp.arange(KEYVALUE_HEADS, dtype=jnp.int32)
    kv_slots = slotted_heads.shape[0]
    chooser = (head_of[:, None] == slotted_heads[None, :]).astype(jnp.bfloat16)
    keys_everywhere = lax.all_gather(keyval_group, "blk", axis=0, tiled=True).reshape(
        sequence_length, 2, kv_slots, HEAD_SIZE
    )
    key_heads = jnp.einsum(
        "hn,lnd->hld", chooser, keys_everywhere[:, 0], preferred_element_type=jnp.float32
    ).astype(jnp.bfloat16)
    value_heads = jnp.einsum(
        "hn,lnd->hld", chooser, keys_everywhere[:, 1], preferred_element_type=jnp.float32
    ).astype(jnp.bfloat16)
    doc_row = documents[0]
    group_start = block_index * group_rows
    query_ids = lax.dynamic_slice_in_dim(doc_row, group_start, group_rows, 0)
    query_pos = group_start + jnp.arange(group_rows, dtype=jnp.int32)

    def block_scores(key_block):
        key_start = key_block * group_rows
        keys_here = lax.dynamic_slice_in_dim(key_heads, key_start, group_rows, 1)
        values_here = lax.dynamic_slice_in_dim(value_heads, key_start, group_rows, 1)
        key_ids = lax.dynamic_slice_in_dim(doc_row, key_start, group_rows, 0)
        key_pos = key_start + jnp.arange(group_rows, dtype=jnp.int32)
        raw_scores = (
            jnp.einsum("qhd,hkd->hqk", query_group, keys_here, preferred_element_type=jnp.float32)
            * score_scale
        )
        allowed = (key_pos[None, :] <= query_pos[:, None]) & (
            key_ids[None, :] == query_ids[:, None]
        )
        return (jnp.where(allowed[None], raw_scores, MASKED_SCORE), keys_here, values_here)

    def forward_step(state, key_block):

        def forward_compute_block(state_in):
            running_max, denom_sum, weighted = state_in
            scores, keys_here, values_here = block_scores(key_block)
            new_max = jnp.maximum(running_max, jnp.max(scores, axis=-1))
            factor = jnp.exp(running_max - new_max)
            unscaled = jnp.exp(scores - new_max[..., None])
            denom_sum = denom_sum * factor + jnp.sum(unscaled, axis=-1)
            weighted = weighted * factor.T[..., None] + jnp.einsum(
                "hqk,hkd->qhd",
                unscaled.astype(jnp.bfloat16),
                values_here,
                preferred_element_type=jnp.float32,
            )
            return (new_max, denom_sum, weighted)

        def forward_skip_block(state_in):
            return state_in

        return (
            lax.cond(key_block <= block_index, forward_compute_block, forward_skip_block, state),
            None,
        )

    start_state = (
        jnp.full((local_heads, group_rows), MASKED_SCORE, jnp.float32),
        jnp.zeros((local_heads, group_rows), jnp.float32),
        jnp.zeros((group_rows, local_heads, HEAD_SIZE), jnp.float32),
    )
    final_state, _ = lax.scan(forward_step, start_state, jnp.arange(block_count, dtype=jnp.int32))
    running_max, denom_sum, weighted = final_state
    log_total = running_max + jnp.log(denom_sum)
    mixed_group = (weighted / denom_sum.T[..., None]).astype(jnp.bfloat16)
    mixed_rows = lax.all_to_all(
        mixed_group.reshape(head_count, sequence_rows, 1, local_heads * HEAD_SIZE),
        "head",
        split_axis=0,
        concat_axis=2,
        tiled=True,
    ).reshape(sequence_rows, QUERY_HEADS * HEAD_SIZE)
    residual_one = x_float + jnp.dot(mixed_rows, weight_o, preferred_element_type=jnp.float32)
    normed_two = rms_scale(residual_one, gain_two).astype(jnp.bfloat16)
    logits = jnp.dot(normed_two, weight_r, preferred_element_type=jnp.float32)
    token_routes = routes[0]
    onehot = (token_routes[..., None] == jnp.arange(expert_count, dtype=jnp.int32)).astype(
        jnp.float32
    )
    chosen = jnp.einsum("tke,te->tk", onehot, logits, precision=EXACT)
    gate_probs = jax.nn.softmax(chosen, axis=-1)
    flat_routes = token_routes.reshape(-1)
    flat_hot = (flat_routes[:, None] == jnp.arange(expert_count, dtype=jnp.int32)).astype(jnp.int32)
    slot_index = jnp.sum((jnp.cumsum(flat_hot, axis=0) - flat_hot) * flat_hot, axis=1)
    dest_rows = flat_routes * capacity + slot_index
    send_rows = (
        jnp.zeros((expert_count * capacity, model_width), jnp.bfloat16)
        .at[dest_rows]
        .set(jnp.repeat(normed_two, TOP, axis=0))
    )
    send_rows = send_rows.reshape(block_count, local_experts, capacity, model_width)
    received = lax.all_to_all(send_rows, "blk", split_axis=0, concat_axis=0, tiled=True)
    gate_up = jnp.einsum("nesd,edf->nesf", received, weight_in, preferred_element_type=jnp.float32)
    active = gated_unit(gate_up).astype(jnp.bfloat16)
    produced = jnp.einsum(
        "nesf,efd->nesd", active, weight_out, preferred_element_type=jnp.float32
    ).astype(jnp.bfloat16)
    returned = lax.all_to_all(produced, "blk", split_axis=0, concat_axis=0, tiled=True)
    picked = returned.reshape(expert_count * capacity, model_width)[dest_rows].reshape(
        sequence_rows, TOP, model_width
    )
    picked_float = picked.astype(jnp.float32)
    expert_mix = jnp.einsum("tk,tkd->td", gate_probs, picked_float, precision=EXACT)
    block_out = (residual_one + expert_mix).astype(jnp.bfloat16)[None]
    out_grad = cotangent[0].astype(jnp.float32)
    gate_grads = jnp.sum(picked_float * out_grad[:, None, :], axis=-1)
    route_grads = (gate_probs[..., None] * out_grad[:, None, :]).astype(jnp.bfloat16)
    grad_send = (
        jnp.zeros((expert_count * capacity, model_width), jnp.bfloat16)
        .at[dest_rows]
        .set(route_grads.reshape(sequence_rows * TOP, model_width))
    )
    grad_recv = lax.all_to_all(
        grad_send.reshape(block_count, local_experts, capacity, model_width),
        "blk",
        split_axis=0,
        concat_axis=0,
        tiled=True,
    )
    active, pull_unit = jax.vjp(gated_unit, gate_up)
    active_low = active.astype(jnp.bfloat16)
    active_grad = jnp.einsum(
        "nesd,efd->nesf", grad_recv, weight_out, preferred_element_type=jnp.float32
    )
    gate_up_grad = pull_unit(active_grad)[0].astype(jnp.bfloat16)
    grad_expert_out = jnp.einsum(
        "nesf,nesd->efd", active_low, grad_recv, preferred_element_type=jnp.float32
    )
    grad_expert_in = jnp.einsum(
        "nesd,nesf->edf", received, gate_up_grad, preferred_element_type=jnp.float32
    )
    input_grad = jnp.einsum(
        "nesf,edf->nesd", gate_up_grad, weight_in, preferred_element_type=jnp.float32
    ).astype(jnp.bfloat16)
    input_back = lax.all_to_all(input_grad, "blk", split_axis=0, concat_axis=0, tiled=True)
    copies = input_back.reshape(expert_count * capacity, model_width)[dest_rows].reshape(
        sequence_rows, TOP, model_width
    )
    normed_two_grad = jnp.sum(copies.astype(jnp.float32), axis=1)
    chosen_grad = gate_probs * (
        gate_grads - jnp.sum(gate_probs * gate_grads, axis=-1, keepdims=True)
    )
    logit_grad = jnp.einsum("tk,tke->te", chosen_grad, onehot, precision=EXACT).astype(jnp.bfloat16)
    grad_router = jnp.einsum(
        "td,te->de", normed_two, logit_grad, preferred_element_type=jnp.float32
    )
    normed_two_grad = normed_two_grad + jnp.einsum(
        "te,de->td", logit_grad, weight_r, preferred_element_type=jnp.float32
    )
    _, pull_two = jax.vjp(rms_scale, residual_one, gain_two)
    residual_part, grad_gain_two = pull_two(normed_two_grad)
    residual_grad = out_grad + residual_part
    attn_grad = residual_grad.astype(jnp.bfloat16)
    grad_output = jnp.einsum("tc,td->cd", mixed_rows, attn_grad, preferred_element_type=jnp.float32)
    mixed_grad = jnp.einsum(
        "td,cd->tc", attn_grad, weight_o, preferred_element_type=jnp.float32
    ).astype(jnp.bfloat16)
    mixed_grad_group = lax.all_to_all(
        mixed_grad.reshape(sequence_rows, head_count, local_heads * HEAD_SIZE),
        "head",
        split_axis=1,
        concat_axis=0,
        tiled=True,
    ).reshape(group_rows, local_heads, HEAD_SIZE)
    delta = jnp.sum(
        mixed_grad_group.astype(jnp.float32) * mixed_group.astype(jnp.float32), axis=-1
    ).T
    chooser_float = chooser.astype(jnp.float32)

    def backward_step(query_acc, key_block):

        def backward_compute_block(grad_in):
            scores, keys_here, values_here = block_scores(key_block)
            prob_exact = jnp.exp(scores - log_total[..., None])
            value_grad = jnp.einsum(
                "hqk,qhd->hkd",
                prob_exact.astype(jnp.bfloat16),
                mixed_grad_group,
                preferred_element_type=jnp.float32,
            )
            prob_grad = jnp.einsum(
                "qhd,hkd->hqk", mixed_grad_group, values_here, preferred_element_type=jnp.float32
            )
            score_grad = (prob_exact * (prob_grad - delta[..., None])).astype(jnp.bfloat16)
            grad_out = (
                grad_in
                + jnp.einsum(
                    "hqk,hkd->qhd", score_grad, keys_here, preferred_element_type=jnp.float32
                )
                * score_scale
            )
            key_grad = (
                jnp.einsum(
                    "hqk,qhd->hkd", score_grad, query_group, preferred_element_type=jnp.float32
                )
                * score_scale
            )
            return (grad_out, key_grad, value_grad)

        def backward_skip_block(grad_in):
            empty = jnp.zeros((local_heads, group_rows, HEAD_SIZE), jnp.float32)
            return (grad_in, empty, empty)

        query_next, key_grad, value_grad = lax.cond(
            key_block <= block_index, backward_compute_block, backward_skip_block, query_acc
        )
        slot_grads = jnp.stack(
            [
                jnp.einsum("hn,hkd->knd", chooser_float, key_grad, precision=EXACT),
                jnp.einsum("hn,hkd->knd", chooser_float, value_grad, precision=EXACT),
            ],
            axis=1,
        )
        return (query_next, slot_grads)

    query_acc, slot_grads = lax.scan(
        backward_step,
        jnp.zeros((group_rows, local_heads, HEAD_SIZE), jnp.float32),
        jnp.arange(block_count, dtype=jnp.int32),
    )
    summed_keys = lax.psum_scatter(
        slot_grads.reshape(sequence_length, 2 * kv_slots * HEAD_SIZE).astype(jnp.bfloat16),
        "blk",
        scatter_dimension=0,
        tiled=True,
    ).astype(jnp.float32)
    query_back, keyval_back = (
        lax.all_to_all(
            query_acc.reshape(head_count, sequence_rows, 1, local_heads * HEAD_SIZE).astype(
                jnp.bfloat16
            ),
            "head",
            split_axis=0,
            concat_axis=2,
            tiled=True,
        ).astype(jnp.float32),
        lax.all_to_all(
            summed_keys.reshape(head_count, sequence_rows, 1, keyvalue_width).astype(jnp.bfloat16),
            "head",
            split_axis=0,
            concat_axis=2,
            tiled=True,
        ).astype(jnp.float32),
    )
    query_pre_grad = (
        apply_rotary(
            query_back.reshape(sequence_rows, QUERY_HEADS, HEAD_SIZE), token_positions, -1.0
        )
        .reshape(sequence_rows, QUERY_HEADS * HEAD_SIZE)
        .astype(jnp.bfloat16)
    )
    keyvalue_sum = jnp.sum(keyval_back[0], axis=1)
    prerotation_key_grad = apply_rotary(
        keyvalue_sum[:, : KEYVALUE_HEADS * HEAD_SIZE].reshape(
            sequence_rows, KEYVALUE_HEADS, HEAD_SIZE
        ),
        token_positions,
        -1.0,
    ).reshape(sequence_rows, KEYVALUE_HEADS * HEAD_SIZE)
    prerotation_keyvalue_grad = jnp.concatenate(
        [prerotation_key_grad, keyvalue_sum[:, KEYVALUE_HEADS * HEAD_SIZE :]], axis=1
    ).astype(jnp.bfloat16)
    grad_query = jnp.einsum(
        "td,te->de", normed_one, query_pre_grad, preferred_element_type=jnp.float32
    )
    grad_keyval = jnp.einsum(
        "td,te->de", normed_one, prerotation_keyvalue_grad, preferred_element_type=jnp.float32
    )
    normed_one_grad = jnp.einsum(
        "te,de->td", query_pre_grad, weight_q, preferred_element_type=jnp.float32
    ) + jnp.einsum(
        "te,de->td", prerotation_keyvalue_grad, weight_kv, preferred_element_type=jnp.float32
    )
    _, pull_one = jax.vjp(rms_scale, x_float, gain_one)
    token_part, grad_gain_one = pull_one(normed_one_grad)
    tokens_grad = (residual_grad + token_part).astype(jnp.bfloat16)[None]
    shared = (
        lax.psum_scatter(grad_gain_one, "fsdp", scatter_dimension=0, tiled=True).astype(
            jnp.float32
        ),
        lax.psum_scatter(
            grad_query.astype(jnp.bfloat16), "fsdp", scatter_dimension=0, tiled=True
        ).astype(jnp.float32),
        lax.psum_scatter(
            grad_keyval.astype(jnp.bfloat16), "fsdp", scatter_dimension=0, tiled=True
        ).astype(jnp.float32),
        lax.psum_scatter(
            grad_output.astype(jnp.bfloat16), "fsdp", scatter_dimension=0, tiled=True
        ).astype(jnp.float32),
        lax.psum_scatter(grad_gain_two, "fsdp", scatter_dimension=0, tiled=True).astype(
            jnp.float32
        ),
        lax.psum_scatter(
            grad_router.astype(jnp.bfloat16), "fsdp", scatter_dimension=0, tiled=True
        ).astype(jnp.float32),
        lax.psum_scatter(
            grad_expert_in.astype(jnp.bfloat16), "fsdp", scatter_dimension=1, tiled=True
        ).astype(jnp.float32),
        lax.psum_scatter(
            grad_expert_out.astype(jnp.bfloat16), "fsdp", scatter_dimension=2, tiled=True
        ).astype(jnp.float32),
    )
    dense = lax.psum(
        (shared[0], shared[1], shared[2], shared[3], shared[4], shared[5]), ("blk", "head")
    )
    expert_sums = (
        lax.psum(shared[6].astype(jnp.bfloat16), "head").astype(jnp.float32),
        lax.psum(shared[7].astype(jnp.bfloat16), "head").astype(jnp.float32),
    )
    return (
        block_out,
        tokens_grad,
        dense[0],
        dense[1],
        dense[2],
        dense[3],
        dense[4],
        dense[5],
        expert_sums[0],
        expert_sums[1],
    )


def solution(mesh):
    placed = (
        P("fsdp", ("blk", "head"), None),
        P("fsdp", None),
        P("fsdp", ("blk", "head"), None),
        P("fsdp", ("blk", "head"), None),
        P("fsdp"),
        P("fsdp", None),
        P("fsdp", None),
        P("fsdp", None),
        P("fsdp"),
        P("fsdp", None),
        P("blk", "fsdp", None),
        P("blk", None, "fsdp"),
    )
    return jax.shard_map(
        on_device,
        mesh=mesh,
        in_specs=placed,
        out_specs=(
            P("fsdp", ("blk", "head"), None),
            P("fsdp", ("blk", "head"), None),
            P("fsdp"),
            P("fsdp", None),
            P("fsdp", None),
            P("fsdp", None),
            P("fsdp"),
            P("fsdp", None),
            P("blk", "fsdp", None),
            P("blk", None, "fsdp"),
        ),
        check_vma=False,
    )
```

profile of v0, /device:TPU:27, one launch (start us, length us, event | category | flops | bytes accessed | tf_op | source)
XLA Modules:
  0.0 1885.8 jit_solution(3657927915679907760)
XLA Ops:
  14.1 23.7 %all-gather.9.cloned.1.call-done = bf16[1536,512]{1,0:T(8,128)(2,1)} async-done(((bf16[768,512]{1,0:T(8,128)(2,1)}), bf16[1536,512]{1,0:T(8,128)(2,1)}) %all-gather.9.cloned.1.call-update) | async-done | bytes 1572880 | tf_op jit(solution)/shard_map/all_gather | solution.py:64
  41.0 16.5 all_to_all.98
  59.0 43.0 %all-gather.13.cloned.1.call-done = bf16[1536,1536]{1,0:T(8,128)(2,1)} async-done(((bf16[768,1536]{1,0:T(8,128)(2,1)}), bf16[1536,1536]{1,0:T(8,128)(2,1)}) %all-gather.13.cloned.1.call-update) | async-done | bytes 4718608 | tf_op jit(solution)/shard_map/all_gather | solution.py:63
  130.4 51.7 %all-gather.11.cloned.1.call-done = bf16[4096,512]{1,0:T(8,128)(2,1)} async-done(((bf16[1024,512]{1,0:T(8,128)(2,1)}), bf16[4096,512]{1,0:T(8,128)(2,1)}) %all-gather.11.cloned.1.call-update) | async-done | bytes 4194320 | tf_op jit(solution)/shard_map/all_gather | solution.py:133
  223.3 70.3 %while.31 = (s32[]{:T(128)}, f32[3,1024]{1,0:T(4,128)S(1)}, f32[3,1024]{1,0:T(4,128)S(1)}, f32[1024,3,128]{0,2,1:T(8,128)}, s32[4]{0:T(128)S(1)}, /*index=5*/s32...) while((s32[]{:T(128)}, f32[3,1024]{1,0:T(4,128)S(1)}, ...), condition=%wide.region_6.7_spmd.clone, body=%wide.region_1.6_spmd.clone.sunk | while | flops 1649159168 | bytes 51880320 | solution.py:192
  242.0 16.4 conditional.6
  259.7 16.4 conditional.6
  338.8 25.7 %all-gather.17.cloned.1.call-done = bf16[2,1536,1536]{2,1,0:T(8,128)(2,1)} async-done(((bf16[2,768,1536]{2,1,0:T(8,128)(2,1)}), bf16[2,1536,1536]{2,1,0:T(8,128)(2,1)}) %all-gather.17.cloned.1.call-update) | async-done | bytes 9437200 | tf_op jit(solution)/shard_map/all_gather | solution.py:68
  364.4 75.0 %all-to-all-done.3 = bf16[4,2,192,1536]{3,2,1,0:T(8,128)(2,1)} async-done(((bf16[4,2,192,1536]{3,2,1,0:T(8,128)(2,1)}), bf16[4,2,192,1536]{3,2,1,0:T(8,128)(2,1)}, u32[]{:S(2)}, u32[]{:S(2)}) %all-to-all-start.3) | async-done | bytes 4718624 | tf_op jit(solution)/shard_map/all_to_all | solution.py:222
  491.8 82.0 %all-to-all-done.4 = bf16[4,2,192,1536]{3,2,1,0:T(8,128)(2,1)} async-done(((bf16[4,2,192,1536]{3,2,1,0:T(8,128)(2,1)}), bf16[4,2,192,1536]{3,2,1,0:T(8,128)(2,1)}, u32[]{:S(2)}, u32[]{:S(2)}) %all-to-all-start.4) | async-done | bytes 4718624 | tf_op jit(solution)/shard_map/all_to_all | solution.py:228
  604.5 109.3 %all_to_all.99 = bf16[4,2,192,1536]{3,2,1,0:T(8,128)(2,1)S(1)} all-to-all(bf16[4,2,192,1536]{3,2,1,0:T(8,128)(2,1)} %bitcast.298), channel_id=1, replica_groups=mesh['blk'=4,'head'=4,'fsdp'=2] {'blk'}, dimensions={0} | all-to-all | bytes 9437184 | tf_op jit(solution)/shard_map/all_to_all | solution.py:243
  762.6 91.6 %all-to-all-done.6 = bf16[4,2,192,1536]{3,2,1,0:T(8,128)(2,1)} async-done(((bf16[4,2,192,1536]{3,2,1,0:T(8,128)(2,1)}), bf16[4,2,192,1536]{3,2,1,0:T(8,128)(2,1)}, u32[]{:S(2)}, u32[]{:S(2)}) %all-to-all-start.6) | async-done | bytes 4718624 | tf_op jit(solution)/shard_map/all_to_all | solution.py:265
  908.1 180.7 %while.32 = (s32[]{:T(128)}, f32[1024,3,128]{0,2,1:T(8,128)S(1)}, bf16[4,1024,2,2,128]{4,3,1,2,0:T(2,128)(2,1)}, s32[4]{0:T(128)S(1)}, s32[]{:T(128)}, /*index=5...) while((s32[]{:T(128)}, f32[1024,3,128]{0,2,1:T(8,128)S(1)}, ...), condition=%wide.region_23.24_spmd.clone, body=%wide.region_20.23_spmd.clone.sunk | while | flops 4083288064 | bytes 109392808 | solution.py:346
  909.5 31.3 %conditional.7 = (f32[1024,3,128]{0,2,1:T(8,128)S(1)}, f32[3,1024,128]{2,0,1:T(4,128)}, f32[3,1024,128]{2,0,1:T(4,128)}) conditional(s32[]{:T(128)} %convert_element_type.499, f32[1024,3,128]{0,2,1:T(8,128)S(1)} %get-tuple-element.762, (s32[]{:T(128)}, bf16[3,4096,128]{2,1,0:T(8,128)(2,1)}, s32[]{:T(128)}, s32[4096]{0:T(1024)S(1)}, ...), branch_computations={%region_21.21_spmd, %region_22.22_spmd} | conditional | flops 4062316544 | bytes 103096440 | solution.py:334
  954.5 31.3 %conditional.7 = (f32[1024,3,128]{0,2,1:T(8,128)S(1)}, f32[3,1024,128]{2,0,1:T(4,128)}, f32[3,1024,128]{2,0,1:T(4,128)}) conditional(s32[]{:T(128)} %convert_element_type.499, f32[1024,3,128]{0,2,1:T(8,128)S(1)} %get-tuple-element.762, (s32[]{:T(128)}, bf16[3,4096,128]{2,1,0:T(8,128)(2,1)}, s32[]{:T(128)}, s32[4096]{0:T(1024)S(1)}, ...), branch_computations={%region_21.21_spmd, %region_22.22_spmd} | conditional | flops 4062316544 | bytes 103096440 | solution.py:334
  999.6 31.3 %conditional.7 = (f32[1024,3,128]{0,2,1:T(8,128)S(1)}, f32[3,1024,128]{2,0,1:T(4,128)}, f32[3,1024,128]{2,0,1:T(4,128)}) conditional(s32[]{:T(128)} %convert_element_type.499, f32[1024,3,128]{0,2,1:T(8,128)S(1)} %get-tuple-element.762, (s32[]{:T(128)}, bf16[3,4096,128]{2,1,0:T(8,128)(2,1)}, s32[]{:T(128)}, s32[4096]{0:T(1024)S(1)}, ...), branch_computations={%region_21.21_spmd, %region_22.22_spmd} | conditional | flops 4062316544 | bytes 103096440 | solution.py:334
  1044.6 31.3 %conditional.7 = (f32[1024,3,128]{0,2,1:T(8,128)S(1)}, f32[3,1024,128]{2,0,1:T(4,128)}, f32[3,1024,128]{2,0,1:T(4,128)}) conditional(s32[]{:T(128)} %convert_element_type.499, f32[1024,3,128]{0,2,1:T(8,128)S(1)} %get-tuple-element.762, (s32[]{:T(128)}, bf16[3,4096,128]{2,1,0:T(8,128)(2,1)}, s32[]{:T(128)}, s32[4096]{0:T(1024)S(1)}, ...), branch_computations={%region_21.21_spmd, %region_22.22_spmd} | conditional | flops 4062316544 | bytes 103096440 | solution.py:334
  1156.6 24.3 %reduce-scatter.8.cloned.1.call-done = bf16[1024,512]{1,0:T(8,128)(2,1)} async-done(((bf16[4096,512]{1,0:T(8,128)(2,1)}), bf16[1024,512]{1,0:T(8,128)(2,1)}) %reduce-scatter.8.cloned.1.call-update) | async-done | bytes 1048592 | tf_op jit(solution)/shard_map/reduce_scatter | solution.py:351
  1200.8 44.1 %reduce-scatter.20.cloned.1.call-done = bf16[2,768,768]{2,1,0:T(8,128)(2,1)} async-done(((bf16[2,768,1536]{2,1,0:T(8,128)(2,1)}), bf16[2,768,768]{2,1,0:T(8,128)(2,1)}) %reduce-scatter.20.cloned.1.call-update) | async-done | bytes 2359312 | tf_op jit(solution)/shard_map/reduce_scatter | solution.py:429
  1244.9 113.5 %reduce-scatter.18.cloned.1.call-done = bf16[2,768,1536]{2,1,0:T(8,128)(2,1)} async-done(((bf16[2,1536,1536]{2,1,0:T(8,128)(2,1)}), bf16[2,768,1536]{2,1,0:T(8,128)(2,1)}) %reduce-scatter.18.cloned.1.call-update) | async-done | bytes 4718608 | tf_op jit(solution)/shard_map/reduce_scatter | solution.py:426
  1375.2 58.5 %reduce-scatter.14.cloned.1.call-done = bf16[768,1536]{1,0:T(8,128)(2,1)} async-done(((bf16[1536,1536]{1,0:T(8,128)(2,1)}), bf16[768,1536]{1,0:T(8,128)(2,1)}) %reduce-scatter.14.cloned.1.call-update) | async-done | bytes 2359312 | tf_op jit(solution)/shard_map/reduce_scatter | solution.py:417
  1444.1 52.4 %reduce-scatter.10.cloned.1.call-done = bf16[768,1536]{1,0:T(8,128)(2,1)} async-done(((bf16[1536,1536]{1,0:T(8,128)(2,1)}), bf16[768,1536]{1,0:T(8,128)(2,1)}) %reduce-scatter.10.cloned.1.call-update) | async-done | bytes 2359312 | tf_op jit(solution)/shard_map/reduce_scatter | solution.py:411
  1496.6 28.4 %reduce-scatter.12.cloned.1.call-done = bf16[768,512]{1,0:T(8,128)(2,1)} async-done(((bf16[1536,512]{1,0:T(8,128)(2,1)}), bf16[768,512]{1,0:T(8,128)(2,1)}) %reduce-scatter.12.cloned.1.call-update) | async-done | bytes 786448 | tf_op jit(solution)/shard_map/reduce_scatter | solution.py:414
  1524.9 344.0 %all-reduce.11 = (f32[768]{0:T(1024)}, f32[768,1536]{1,0:T(8,128)}, f32[768,512]{1,0:T(8,128)}, f32[768,1536]{1,0:T(8,128)}, f32[768]{0:T(1024)}, /*index=5*/f32[768,8]{0,1:T(8,128)}) all-reduce(f32[768]{0:T(1024)S(1)} %get-tuple-element.517, ...), channel_id=1, replica_groups=mesh['blk'=4,'head'=4,'fsdp'=2] {'blk','head'}, use_global_device_ids=true, to_apply=%region_29.30 | all-reduce | flops 2760192 | bytes 16564224 | tf_op jit(solution)/shard_map/psum | solution.py:433
  (386 shorter events, 707.3 us)
Async XLA Ops:
  7.2 30.6 %all-gather.9.cloned.1.call-start = ((), (), s32[]{:S(2)}) async-start(), calls=%async_computation.17 | async-start | bytes 2359296 | tf_op jit(solution)/shard_map/all_gather | solution.py:64
  7.9 94.1 %all-gather.13.cloned.1.call-start = ((), (), s32[]{:S(2)}) async-start(), calls=%async_computation.19 | async-start | bytes 7077888 | tf_op jit(solution)/shard_map/all_gather | solution.py:63
  8.7 173.4 %all-gather.11.cloned.1.call-start = ((), (), s32[]{:S(2)}) async-start(), calls=%async_computation.18 | async-start | bytes 5242880 | tf_op jit(solution)/shard_map/all_gather | solution.py:133
  57.6 253.7 %all-gather.15.cloned.1.call-start = ((), (), s32[]{:S(2)}) async-start(), calls=%async_computation.20 | async-start | bytes 7077888 | tf_op jit(solution)/shard_map/all_gather | solution.py:65
  58.2 306.3 %all-gather.17.cloned.1.call-start = ((), (), s32[]{:S(2)}) async-start(), calls=%async_computation.21 | async-start | bytes 14155776 | tf_op jit(solution)/shard_map/all_gather | solution.py:68
  113.8 14.3 all-to-all-start.1
  296.7 13.9 all-to-all-start.2
  315.6 174.5 %copy-start.11 = (bf16[256,1536]{1,0:T(8,128)(2,1)}, bf16[256,1536]{1,0:T(8,128)(2,1)S(1)}, u32[]{:S(2)}) copy-start(bf16[256,1536]{1,0:T(8,128)(2,1)S(1)} %multiply_convert_fusion.3) | copy-start | bytes 2359300
  333.2 106.2 %all-to-all-start.3 = ((bf16[4,2,192,1536]{3,2,1,0:T(8,128)(2,1)}), bf16[4,2,192,1536]{3,2,1,0:T(8,128)(2,1)}, u32[]{:S(2)}, u32[]{:S(2)}) async-start(bf16[4,2,192,1536]{3,2,1,0:T(8,128)(2,1)} %bitcast.297), calls=%async_computation.3 | async-start | bytes 9437184 | tf_op jit(solution)/shard_map/all_to_all | solution.py:222
  338.2 118.4 %all-gather.19.cloned.1.call-start = ((), (), s32[]{:S(2)}) async-start(), calls=%async_computation.22 | async-start | bytes 7077888 | tf_op jit(solution)/shard_map/all_gather | solution.py:69
  465.9 107.9 %all-to-all-start.4 = ((bf16[4,2,192,1536]{3,2,1,0:T(8,128)(2,1)}), bf16[4,2,192,1536]{3,2,1,0:T(8,128)(2,1)}, u32[]{:S(2)}, u32[]{:S(2)}) async-start(bf16[4,2,192,1536]{3,2,1,0:T(8,128)(2,1)} %copy.131), calls=%async_computation.4 | async-start | bytes 9437184 | tf_op jit(solution)/shard_map/all_to_all | solution.py:228
  747.2 107.0 %all-to-all-start.6 = ((bf16[4,2,192,1536]{3,2,1,0:T(8,128)(2,1)}), bf16[4,2,192,1536]{3,2,1,0:T(8,128)(2,1)}, u32[]{:S(2)}, u32[]{:S(2)}) async-start(bf16[4,2,192,1536]{3,2,1,0:T(8,128)(2,1)} %copy.133), calls=%async_computation.6 | async-start | bytes 9437184 | tf_op jit(solution)/shard_map/all_to_all | solution.py:265
  886.9 16.9 all-to-all-start.7
  894.1 286.8 %reduce-scatter.8.cloned.1.call-start = ((), (), s32[]{:S(2)}) async-start(), calls=%async_computation.23 | async-start | bytes 5242880 | tf_op jit(solution)/shard_map/reduce_scatter | solution.py:351
  1103.1 141.8 %reduce-scatter.20.cloned.1.call-start = ((), (), s32[]{:S(2)}) async-start(), calls=%async_computation.29 | async-start | bytes 7077888 | tf_op jit(solution)/shard_map/reduce_scatter | solution.py:429
  1112.5 245.8 %reduce-scatter.18.cloned.1.call-start = ((), (), s32[]{:S(2)}) async-start(), calls=%async_computation.28 | async-start | bytes 14155776 | tf_op jit(solution)/shard_map/reduce_scatter | solution.py:426
  1127.0 243.3 %reduce-scatter.16.cloned.1.call-start = ((), (), s32[]{:S(2)}) async-start(), calls=%async_computation.27 | async-start | bytes 36864 | tf_op jit(solution)/shard_map/reduce_scatter | solution.py:423
  1129.8 303.8 %reduce-scatter.14.cloned.1.call-start = ((), (), s32[]{:S(2)}) async-start(), calls=%async_computation.26 | async-start | bytes 7077888 | tf_op jit(solution)/shard_map/reduce_scatter | solution.py:417
  1135.1 361.5 %reduce-scatter.10.cloned.1.call-start = ((), (), s32[]{:S(2)}) async-start(), calls=%async_computation.24 | async-start | bytes 7077888 | tf_op jit(solution)/shard_map/reduce_scatter | solution.py:411
  1180.9 16.7 all-to-all-start.9
  1185.0 339.9 %reduce-scatter.12.cloned.1.call-start = ((), (), s32[]{:S(2)}) async-start(), calls=%async_computation.25 | async-start | bytes 2359296 | tf_op jit(solution)/shard_map/reduce_scatter | solution.py:414
  1200.7 157.7 %copy-start.37 = (u32[32]{0:T(128)S(1)}, u32[32]{0:T(128)}, u32[]{:S(2)}) copy-start(u32[32]{0:T(128)} %constant.135) | copy-start | bytes 388
  1200.7 668.2 %all-reduce.10.cloned.1.call-start = ((), (), s32[]{:S(2)}) async-start(), calls=%async_computation.30 | async-start | bytes 14155776 | tf_op jit(solution)/shard_map/psum | solution.py:437
  1375.2 149.7 %copy-start.32 = (bf16[768,8]{0,1:T(8,128)(2,1)S(1)}, bf16[768,8]{0,1:T(8,128)(2,1)}, u32[]{:S(2)}) copy-start(bf16[768,8]{0,1:T(8,128)(2,1)} %reduce-scatter.16.cloned.1.call-done) | copy-start | bytes 36868
  (43 other events, 1026.7 us)
Sparse Core Ops, SparseCore 0:
  9.6 28.1 all-gather.8
  39.3 62.6 all-gather.12
  103.6 78.4 all-gather.10
  183.5 63.4 all-gather.14
  248.4 116.0 all-gather.16
  365.8 62.6 all-gather.18
  1103.2 77.5 reduce-scatter.7
  1183.9 60.9 reduce-scatter.19
  1247.8 110.5 reduce-scatter.17
  1360.9 9.2 reduce-scatter.15
  1373.2 60.4 reduce-scatter.13
  1436.5 59.9 reduce-scatter.9
  1498.8 26.0 reduce-scatter.11
  1527.4 253.5 all-reduce.9
where the time goes:
time: 1900 us; the launch traced here: 1890 us
  waiting for transfers between devices  758 us (40%)
  blocking collectives  499 us (26%)
  matrix products  305 us (16%)
  local copies, waits for them, and re-layouts  171 us (9%)
  other arithmetic  87.1 us (5%)
  starting transfers between devices  39.2 us (2%)
    psum x1, blocking collectives, on_device(): lax.psum((shared[0], shared[1], shared[2], shared[3], shared[4], shared[5...  344 us
    reduce_scatter x1, waiting for transfers between devices, on_device(): lax.psum_scatter(grad_expert_in.astype(jnp.bfloat16), 'fsdp', scatter_dim...  113 us
    all_to_all x1, blocking collectives, on_device(): lax.all_to_all(grad_send.reshape(block_count, local_experts, capacity, mo...  109 us
    all_to_all x1, waiting for transfers between devices, on_device(): lax.all_to_all(input_grad, 'blk', split_axis=0, concat_axis=0, tiled=True)  91.6 us
    all_to_all x1, waiting for transfers between devices, on_device(): lax.all_to_all(produced, 'blk', split_axis=0, concat_axis=0, tiled=True)  82 us
    all_to_all x1, waiting for transfers between devices, on_device(): lax.all_to_all(send_rows, 'blk', split_axis=0, concat_axis=0, tiled=True)  75 us
    reduce_scatter x1, waiting for transfers between devices, on_device(): lax.psum_scatter(grad_output.astype(jnp.bfloat16), 'fsdp', scatter_dimens...  58.5 us
    reduce_scatter x1, waiting for transfers between devices, on_device(): lax.psum_scatter(grad_query.astype(jnp.bfloat16), 'fsdp', scatter_dimensi...  52.4 us
  transfers between devices with their start and end apart: 21, of which 18 were waited for; matrix products, arithmetic and copies ran while one was open for 13% of the time, Pallas kernels for 0%

commit v1 on v0

v1 whole, which is shorter than its diff:
```python
import functools

import jax
import jax.numpy as jnp
from jax import lax
from jax.experimental import pallas as pl
from jax.experimental.pallas import tpu as pltpu
from jax.sharding import PartitionSpec as P

QUERY_HEADS = 12
KEYVALUE_HEADS = 2
HEAD = 128
NORM_EPSILON = 1e-06
ROPE_BASE = 1000000.0
MASKED = -1e30
DOCUMENTS = 4
LOG2E = 1.4426950408889634
SCORE_LOG2 = HEAD ** (-0.5) * LOG2E
SCORE_SCALE = HEAD ** (-0.5)
TILE = 256
BF16 = jnp.bfloat16
F32 = jnp.float32
VMEM_BYTES = 63 * 1024 * 1024

NN = (((1,), (0,)), ((), ()))
NT = (((1,), (1,)), ((), ()))
TN = (((0,), (0,)), ((), ()))


def mm(a, b, dims=NN):
    return lax.dot_general(a, b, dims, preferred_element_type=F32)


def gelu_parts(gate):
    c = 0.7978845608028654
    cube = 0.044715 * gate * gate * gate
    t = jnp.tanh(c * (gate + cube))
    value = 0.5 * gate * (1.0 + t)
    slope = 0.5 * (1.0 + t) + 0.5 * gate * (1.0 - t * t) * c * (1.0 + 3.0 * 0.044715 * gate * gate)
    return value, slope


def score_tile(key_rows, q_tile, start_row, first_key, q_first):
    scores = mm(key_rows, q_tile, NT) * SCORE_LOG2
    key_pos = first_key + lax.broadcasted_iota(jnp.int32, scores.shape, 0)
    allowed = key_pos >= start_row
    if q_first is not None:
        q_pos = q_first + lax.broadcasted_iota(jnp.int32, scores.shape, 1)
        allowed = allowed & (key_pos <= q_pos)
    return jnp.where(allowed, scores, MASKED)


def attend_tile(hh, cols, key_rows, value_cols, q_ref, start_ref, m_ref, l_ref, acc_ref, first_key, q_first):
    q_tile = q_ref[hh, cols, :]
    scores = score_tile(key_rows, q_tile, start_ref[:, cols], first_key, q_first)
    old = m_ref[hh, :, cols]
    new = jnp.maximum(old, jnp.max(scores, axis=0, keepdims=True))
    factor = jnp.exp2(old - new)
    prob = jnp.exp2(scores - new)
    m_ref[hh, :, cols] = new
    l_ref[hh, :, cols] = l_ref[hh, :, cols] * factor + jnp.sum(prob, axis=0, keepdims=True)
    acc_ref[hh, :, cols] = acc_ref[hh, :, cols] * factor + mm(value_cols, prob.astype(BF16))


def unattend_tile(hh, cols, key_rows, value_rows, key_cols, q_ref, do_ref, start_ref, lse_ref, delta_ref,
                  dq_ref, dk_ref, dv_ref, first_key, q_first):
    n = key_rows.shape[0]
    q_tile = q_ref[hh, cols, :]
    do_tile = do_ref[hh, cols, :]
    scores = score_tile(key_rows, q_tile, start_ref[:, cols], first_key, q_first)
    prob = jnp.exp2(scores - lse_ref[hh, :, cols])
    dv_ref[:n, :] += mm(prob.astype(BF16), do_tile)
    prob_grad = mm(value_rows, do_tile, NT)
    score_grad = (prob * (prob_grad - delta_ref[hh, :, cols])).astype(BF16)
    dk_ref[:n, :] += mm(score_grad, q_tile)
    dq_ref[hh, :, cols] += mm(key_cols, score_grad)


def remote(src, dst, send_sem, recv_sem, **to):
    return pltpu.make_async_remote_copy(
        src_ref=src, dst_ref=dst, send_sem=send_sem, recv_sem=recv_sem, device_id=to,
        device_id_type=pl.DeviceIdType.MESH)


class Lanes:
    def __init__(self, send, recv):
        self.send, self.recv, self.used, self.sent, self.pending = send, recv, 0, 0, []

    def slots(self, count=1):
        first = self.used
        self.used += count
        assert self.used <= self.recv.shape[0]
        return first

    def sends(self, count):
        first = self.sent
        self.sent += count
        assert self.sent <= self.send.shape[0]
        return first

    def put(self, slot, src, dst, when=None, **to):
        assert self.sent < self.send.shape[0]
        copy = remote(src, dst, self.send.at[self.sent], self.recv.at[slot], **to)
        self.sent += 1
        if when is None:
            copy.start()
        else:
            pl.when(when)(copy.start)
        self.pending.append((copy, when))
        return self.pending[-1]

    def settle(self, entry):
        copy, when = entry
        self.pending = [other for other in self.pending if other is not entry]
        if when is None:
            copy.wait_send()
        else:
            pl.when(when)(copy.wait_send)

    def arrived(self, slot, dst, when=None, **origin):
        copy = remote(dst, dst, self.send.at[0], self.recv.at[slot], **origin)
        if when is None:
            copy.wait_recv()
        else:
            pl.when(when)(copy.wait_recv)

    def drain(self):
        for copy, when in self.pending:
            if when is None:
                copy.wait_send()
            else:
                pl.when(when)(copy.wait_send)
        self.pending = []


class Place:
    def __init__(self, blocks):
        self.z, self.h, self.y = lax.axis_index("blk"), lax.axis_index("head"), lax.axis_index("fsdp")
        self.blocks = blocks
        self.x, self.c = self.h // 2, self.h % 2
        self.sib = 2 * self.x + 1 - self.c
        self.xn = 2 * (1 - self.x) + self.c
        self.xs = 2 * (1 - self.x) + 1 - self.c
        self.oy = 1 - self.y

    def others(self):
        return [(self.z + d) % self.blocks for d in range(1, self.blocks)]

    def enter(self):
        barrier = pltpu.get_barrier_semaphore()

        def greet(**to):
            pl.semaphore_signal(barrier, inc=1, device_id=to, device_id_type=pl.DeviceIdType.MESH)

        for head in (self.sib, self.xn, self.xs):
            greet(head=head)
        greet(fsdp=self.oy)
        for z in self.others():
            greet(blk=z)
        pl.semaphore_wait(barrier, 4 + self.blocks - 1)


def gather_heads(at, lanes, own, land):
    s = lanes.slots(3)
    rows = own.shape[0]

    def slot(head):
        return land.at[pl.ds(pl.multiple_of(head * rows, rows), rows), :]

    lanes.put(s, own, slot(at.h), head=at.xn)
    lanes.put(s + 1, own, slot(at.h), head=at.sib)

    passed = []

    def forward():
        lanes.arrived(s, slot(at.xn), head=at.xn)
        passed.append(lanes.put(s + 2, slot(at.xn), slot(at.xn), head=at.sib))

    def near():
        lanes.arrived(s + 1, slot(at.sib), head=at.sib)

    def far():
        lanes.arrived(s + 2, slot(at.xs), head=at.sib)

    return forward, near, far, passed


def aligned(index, size):
    return pl.ds(pl.multiple_of(index, 16), size)


def semaphores(blocks):
    count = 128 + 16 * blocks
    return [pltpu.SemaphoreType.DMA((count,)), pltpu.SemaphoreType.DMA((count,))]


class Shared:
    def __init__(self, at, lanes, chunks, give, hold):
        self.at, self.lanes, self.chunks, self.give, self.hold = at, lanes, chunks, give, hold
        self.pieces = len(give(0)) if give else 0
        self.ys = lanes.slots(chunks * self.pieces)
        self.xn, self.sib, self.far = lanes.slots(chunks), lanes.slots(chunks), lanes.slots(chunks)
        self.sent = []

    def begin(self, k):
        for i, (src, dst) in enumerate(self.give(k)):
            self.lanes.put(self.ys + k * self.pieces + i, src, dst(self.at.y), fsdp=self.at.oy)

    def landed(self, k):
        for i, (src, dst) in enumerate(self.give(k)):
            self.lanes.arrived(self.ys + k * self.pieces + i, dst(self.at.oy), fsdp=self.at.oy)

    def spread(self, k):
        self.landed(k)
        self.scatter(k)

    def scatter(self, k):
        at = self.at
        place = self.hold(k, at.h, at.oy)
        self.sent.append(self.lanes.put(self.xn + k, place, place, head=at.xn))
        self.sent.append(self.lanes.put(self.sib + k, place, place, head=at.sib))

    def forward(self, k):
        at = self.at
        place = self.hold(k, at.xn, at.oy)
        self.lanes.arrived(self.xn + k, place, head=at.xn)
        self.sent.append(self.lanes.put(self.far + k, place, place, head=at.sib))

    def settle(self):
        for entry in self.sent:
            self.lanes.settle(entry)

    def finish(self, k):
        at = self.at
        self.lanes.arrived(self.sib + k, self.hold(k, at.sib, at.oy), head=at.sib)
        self.lanes.arrived(self.far + k, self.hold(k, at.xs, at.oy), head=at.sib)


def weight_chunk(w_ref, k, head, y):
    quarter = w_ref.shape[2] // 4
    piece = quarter // 2
    return w_ref.at[k // 2, y, aligned(head * quarter + k % 2 * piece, piece), :]


class Column:
    def __init__(self, at, lanes, land):
        self.at, self.lanes, self.land = at, lanes, land
        self.slot = lanes.slots(at.blocks)

    def begin(self, own):
        at = self.at
        place = self.land.at[at.z]
        self.lanes.put(self.slot + at.z, own, place, when=at.z < at.blocks - 1, blk=at.z + 1)
        self.lanes.put(self.slot + at.z, own, place, when=at.z > 0, blk=at.z - 1)

    def hand_on(self, d):
        at = self.at
        for b, origin, next_z in ((at.z - d, at.z - 1, at.z + 1), (at.z + d, at.z + 1, at.z - 1)):
            there = (b >= 0) & (b < at.blocks)
            safe = jnp.clip(b, 0, at.blocks - 1)
            self.lanes.arrived(self.slot + safe, self.land.at[safe], when=there, blk=origin)
            self.lanes.put(self.slot + safe, self.land.at[safe], self.land.at[safe],
                           when=there & (next_z >= 0) & (next_z < at.blocks), blk=next_z)


def front_kernel(x_ref, small_ref, wq_hbm, wkv_hbm, wo_hbm, win_hbm, wout_hbm, cot_hbm, cos_ref, sin_ref, start_ref,
                 q_ref, o_ref, ot_ref, lse_ref, n1_ref, small_out, wqkv_out, kv_out, wo_out, w_out, cot_out,
                 xg_ref, small_land, wqkv_ref, kv_ref, m_ref, l_ref, acc_ref, vt_ref, wo_ref, w_ref, cot_ref,
                 load_sem, send_sem, recv_sem):
    heads, rows, _ = q_ref.shape
    own_rows, width = x_ref.shape
    blocks = kv_ref.shape[0]
    half = wq_hbm.shape[0]
    qcols = heads * HEAD
    experts = 2 * blocks
    at = Place(blocks)
    me = at.z
    lanes = Lanes(send_sem, recv_sem)
    at.enter()
    local = []

    def copy_here(src, dst):
        copy = pltpu.make_async_copy(src, dst, load_sem.at[len(local)])
        copy.start()
        local.append(copy)
        return copy

    forward, near, far, _ = gather_heads(at, lanes, x_ref, xg_ref)
    g = at.x
    q_from = pl.ds(pl.multiple_of(at.h * qcols, HEAD), qcols)
    k_from = pl.ds(pl.multiple_of(g * HEAD, HEAD), HEAD)
    v_from = pl.ds(pl.multiple_of((KEYVALUE_HEADS + g) * HEAD, HEAD), HEAD)
    columns = ((wq_hbm.at[:, q_from], slice(0, qcols)), (wkv_hbm.at[:, k_from], slice(qcols, qcols + HEAD)),
               (wkv_hbm.at[:, v_from], slice(qcols + HEAD, qcols + 2 * HEAD)))

    def weight_rows(y, cols):
        return wqkv_ref.at[aligned(y * half, half), cols]

    ws = lanes.slots(3)
    for i, (src, cols) in enumerate(columns):
        lanes.put(ws + i, src, weight_rows(at.y, cols), fsdp=at.oy)
    smalls = lanes.slots()
    lanes.put(smalls, small_ref, small_land, fsdp=at.oy)
    own_weights = [copy_here(src, weight_rows(at.y, cols)) for src, cols in columns]
    cots = Column(at, lanes, cot_ref)
    own_half = pl.ds(pl.multiple_of(at.y * half, half), half)
    cot_load = copy_here(cot_hbm, cot_ref.at[me])
    wo_load = copy_here(wo_hbm, wo_ref.at[own_half, :])
    w_loads = [copy_here(win_hbm, w_ref.at[:, at.y, :, :width]), copy_here(wout_hbm, w_ref.at[:, at.y, :, width:])]
    cot_load.wait()
    cots.begin(cot_ref.at[me])

    quarter = half // 4

    def wo_place(k, head, y):
        return wo_ref.at[aligned(y * half + head * quarter, quarter), :]

    shared_wo = Shared(at, lanes, 1,
                       lambda k: [(wo_place(0, at.h, at.y), lambda y: wo_place(0, at.h, y))],
                       wo_place)
    chunks, spread_here = 4, 2

    def w_place(k, head, y):
        return weight_chunk(w_ref, k, head, y)

    def w_give(k):
        return [(w_place(k, at.h, at.y), lambda y: w_place(k, at.h, y))]

    shared_w = Shared(at, lanes, chunks, w_give, w_place)

    small_out[:, :half] = jnp.zeros((small_ref.shape[0], half), BF16)
    lanes.arrived(smalls, small_land, fsdp=at.oy)
    for y in range(2):
        @pl.when(at.y == y)
        def _(y=y):
            small_out[:, y * half:(y + 1) * half] = small_ref[...]
            small_out[:, (1 - y) * half:(2 - y) * half] = small_land[...]

    def norm(head, block):
        x = block.astype(F32)
        inv = lax.rsqrt(jnp.mean(x * x, axis=-1, keepdims=True) + NORM_EPSILON)
        n1_ref[aligned(head * own_rows, own_rows), :] = (x * inv * small_out[experts:experts + 1, :].astype(F32)).astype(BF16)

    def gathered(head):
        return xg_ref[aligned(head * own_rows, own_rows), :]

    norm(at.h, x_ref[...])
    near()
    norm(at.sib, gathered(at.sib))
    forward()
    norm(at.xn, gathered(at.xn))
    far()
    norm(at.xs, gathered(at.xs))
    for copy in own_weights:
        copy.wait()
    for i, (_, cols) in enumerate(columns):
        lanes.arrived(ws + i, weight_rows(at.oy, cols), fsdp=at.oy)
    wo_load.wait()
    shared_wo.begin(0)
    for load in w_loads:
        load.wait()
    for k in range(chunks):
        shared_w.begin(k)
    cots.hand_on(1)

    def project(i, _):
        band = aligned(i * TILE, TILE)
        pre = mm(n1_ref[band, :], wqkv_ref[...])
        cosine, sine = cos_ref[band, :], sin_ref[band, :]

        def turned(u):
            return (u * cosine + pltpu.roll(u, HEAD // 2, 1) * sine).astype(BF16)

        for hh in range(heads):
            q_ref[hh, band, :] = turned(pre[:, hh * HEAD:(hh + 1) * HEAD])
        kv_ref[me, band, :HEAD] = turned(pre[:, qcols:qcols + HEAD])
        kv_ref[me, band, HEAD:] = pre[:, qcols + HEAD:].astype(BF16)
        return 0

    lax.fori_loop(0, rows // TILE, project, 0)

    kvs, kvc = lanes.slots(blocks), lanes.slots(blocks)
    half_rows = rows // 2

    def kv_half(b, core):
        return kv_ref.at[b, aligned(core * half_rows, half_rows), :]

    lanes.put(kvs + me, kv_half(me, at.c), kv_half(me, at.c), when=me < blocks - 1, blk=me + 1)
    late = [copy_here(wqkv_ref, wqkv_out), copy_here(wo_ref.at[own_half, :], wo_out.at[own_half, :]),
            copy_here(w_ref.at[:, at.y], w_out.at[:, at.y])]

    m_ref[...] = jnp.full_like(m_ref, MASKED)
    l_ref[...] = jnp.zeros_like(l_ref)
    acc_ref[...] = jnp.zeros_like(acc_ref)

    def transpose_values(b):
        vt_ref[...] = kv_ref[b, :, HEAD:].astype(F32).T.astype(BF16)

    transpose_values(me)
    for i in range(rows // TILE):
        n = (i + 1) * TILE

        def diagonal(hh, _, i=i, n=n):
            attend_tile(hh, slice(i * TILE, n), kv_ref[me, :n, :HEAD], vt_ref[:, :n], q_ref, start_ref,
                        m_ref, l_ref, acc_ref, me * rows, me * rows + i * TILE)
            return 0

        lax.fori_loop(0, heads, diagonal, 0)

    def block(b):
        transpose_values(b)

        def tile(t, _):
            hh, i = t // (rows // TILE), t % (rows // TILE)
            cols = pl.ds(pl.multiple_of(i * TILE, TILE), TILE)
            attend_tile(hh, cols, kv_ref[b, :, :HEAD], vt_ref[...], q_ref, start_ref,
                        m_ref, l_ref, acc_ref, b * rows, None)
            return 0

        lax.fori_loop(0, heads * (rows // TILE), tile, 0)

    ticks = [[functools.partial(shared_wo.spread, 0), functools.partial(shared_w.spread, 0)],
             [functools.partial(shared_w.spread, 1), functools.partial(shared_wo.forward, 0),
              functools.partial(cots.hand_on, 2)],
             [functools.partial(shared_w.forward, 0)] + [functools.partial(cots.hand_on, d) for d in range(3, blocks)],
             [functools.partial(shared_w.forward, 1)]]

    def tick():
        if ticks:
            for f in ticks.pop(0):
                f()

    for d in range(1, blocks):
        b = jnp.maximum(me - d, 0)
        there = me >= d
        lanes.arrived(kvs + b, kv_half(b, at.c), when=there, blk=me - 1)
        lanes.put(kvs + b, kv_half(b, at.c), kv_half(b, at.c), when=there & (me < blocks - 1), blk=me + 1)
        lanes.put(kvc + b, kv_half(b, at.c), kv_half(b, at.c), when=there, head=at.sib)
        lanes.arrived(kvc + b, kv_half(b, 1 - at.c), when=there, head=at.sib)
        pl.when(there)(functools.partial(block, b))
        tick()

    for hh in range(heads):
        total = l_ref[hh]
        done = acc_ref[hh] / total
        ot_ref[hh * HEAD:(hh + 1) * HEAD, :] = done.astype(BF16)
        o_ref[:, hh * HEAD:(hh + 1) * HEAD] = done.T.astype(BF16)
        lse_ref[hh] = m_ref[hh] + jnp.log2(total)
    kv_copies = [pltpu.make_async_copy(kv_ref.at[b], kv_out.at[b], load_sem.at[15]) for b in range(blocks)]
    for b, copy in enumerate(kv_copies):
        @pl.when(b <= me)
        def _(copy=copy):
            copy.start()
            copy.wait()
    while ticks:
        tick()
    shared_wo.finish(0)
    other_half = pl.ds(pl.multiple_of(at.oy * half, half), half)
    late.append(copy_here(wo_ref.at[other_half, :], wo_out.at[other_half, :]))
    late.append(copy_here(cot_ref, cot_out))
    for k in range(spread_here):
        shared_w.finish(k)
    for k in range(spread_here, chunks):
        shared_w.landed(k)
    late.append(copy_here(w_ref.at[:, at.oy], w_out.at[:, at.oy]))
    for copy in late:
        copy.wait()
    lanes.drain()


def front(blocks, x, small, wq, wkv, wo, win, wout, cot, cosine, sine, start):
    own_rows, width = x.shape
    rows = cosine.shape[0]
    half = wq.shape[0]
    heads = QUERY_HEADS * own_rows // rows
    qcols = heads * HEAD
    ffe = wout.shape[1]
    vm = pl.BlockSpec(memory_space=pltpu.VMEM)
    hbm = pl.BlockSpec(memory_space=pl.ANY)
    sds = jax.ShapeDtypeStruct
    return pl.pallas_call(
        front_kernel,
        out_shape=(
            sds((heads, rows, HEAD), BF16),
            sds((rows, qcols), BF16),
            sds((qcols, rows), BF16),
            sds((heads, 1, rows), F32),
            sds((rows, width), BF16),
            sds((small.shape[0], width), BF16),
            sds((width, qcols + 2 * HEAD), BF16),
            sds((blocks, rows, 2 * HEAD), BF16),
            sds((width, width), BF16),
            sds((2, 2, half, width + half), BF16),
            sds((blocks, own_rows, width), BF16),
        ),
        in_specs=[vm, vm] + [hbm] * 6 + [vm] * 3,
        out_specs=[vm] * 6 + [hbm] * 5,
        scratch_shapes=[
            pltpu.VMEM((rows, width), BF16),
            pltpu.VMEM(small.shape, BF16),
            pltpu.VMEM((width, qcols + 2 * HEAD), BF16),
            pltpu.VMEM((blocks, rows, 2 * HEAD), BF16),
            pltpu.VMEM((heads, 1, rows), F32),
            pltpu.VMEM((heads, 1, rows), F32),
            pltpu.VMEM((heads, HEAD, rows), F32),
            pltpu.VMEM((HEAD, rows), BF16),
            pltpu.VMEM((width, width), BF16),
            pltpu.VMEM((2, 2, half, width + half), BF16),
            pltpu.VMEM((blocks, own_rows, width), BF16),
            pltpu.SemaphoreType.DMA((16,)),
        ] + semaphores(blocks),
        compiler_params=pltpu.CompilerParams(
            vmem_limit_bytes=VMEM_BYTES, collective_id=0, has_side_effects=True),
    )(x, small, wq, wkv, wo, win, wout, cot, cosine, sine, start)


class ColumnSum:
    CHUNKS = 4

    def __init__(self, at, lanes, part, land):
        self.at, self.lanes, self.part, self.land = at, lanes, part, land
        self.rows = part.shape[1] // self.CHUNKS
        self.recv = lanes.slots((at.blocks + 1) * self.CHUNKS)
        self.sent = lanes.sends(at.blocks * self.CHUNKS)

    def copy(self, b, ch):
        at = self.at
        travel = jnp.where(b < at.z, -1, 1)
        there = at.z + travel
        slot = jnp.where((there == b) & (b > at.z), at.blocks, b)
        rows = pl.ds(ch * self.rows, self.rows)
        return remote(self.part.at[b, rows, :], self.land.at[slot, rows, :],
                      self.lanes.send.at[self.sent + b * self.CHUNKS + ch],
                      self.lanes.recv.at[self.recv + slot * self.CHUNKS + ch], blk=there)

    def landed(self, slot, ch, origin):
        rows = pl.ds(ch * self.rows, self.rows)
        place = self.land.at[slot, rows, :]
        remote(place, place, self.lanes.send.at[0], self.lanes.recv.at[self.recv + slot * self.CHUNKS + ch],
               blk=origin).wait_recv()

    def first_send(self, b):
        at = self.at

        @pl.when(((b < at.z) & (at.z == at.blocks - 1)) | ((b > at.z) & (at.z == 0)))
        def _():
            for ch in range(self.CHUNKS):
                self.copy(b, ch).start()

    def relay(self, phase, d, add):
        at = self.at
        s = jnp.where(at.z * 2 >= at.blocks, -1, 1) * (1 - 2 * phase)
        b, origin = at.z + s * d, at.z - s
        safe = jnp.clip(b, 0, at.blocks - 1)

        @pl.when((b >= 0) & (b < at.blocks) & (origin >= 0) & (origin < at.blocks))
        def _():
            for ch in range(self.CHUNKS):
                self.landed(safe, ch, origin)
                add(safe, pl.ds(ch * self.rows, self.rows))
                self.copy(safe, ch).start()

    def arrive(self, side, use):
        at = self.at
        slot, origin = (at.z, at.z + 1) if side == 0 else (at.blocks, at.z - 1)

        @pl.when((origin >= 0) & (origin < at.blocks))
        def _():
            for ch in range(self.CHUNKS):
                self.landed(slot, ch, origin)
            use(slot)

    def finish(self):
        at = self.at
        for b in range(at.blocks):
            @pl.when(b != at.z)
            def _(b=b):
                for ch in range(self.CHUNKS):
                    self.copy(b, ch).wait_send()


LANES = 128
HALF_LANES = LANES // 2


def split_lanes(value):
    high = value.astype(BF16).astype(F32)
    return (high + pltpu.roll(value - high, HALF_LANES, 1)).astype(BF16)


def expert_kernel(o_ref, x_ref, small_ref, chosen_ref, wo_hbm, w_hbm, cot_hbm,
                  res_out, grad_out, attn_out, small_out, sums_out, y_out, core_land, *rest):
    big = cot_hbm.shape[0] > 4
    if big:
        xb_ref, dx_ref, land_ref, *rest = rest
        (xb_stage, dx_stage, land_stage, g_ref, *rest) = rest
    else:
        xb_ref, dx_ref, land_ref, *rest = rest
    (mix_ref, w_ref, cot_ref, acc_ref, gate_ref, dgu_ref, ga_ref, xt_ref, gat_ref, gg_ref, y_ref, stage_ref,
     gates_ref, router_ref, load_sem, y_sem, send_sem, recv_sem) = rest
    own_rows, width = x_ref.shape
    blocks = cot_hbm.shape[0]
    qcols = o_ref.shape[1]
    half = width // 2
    experts, _, ffe, _ = w_ref.shape
    at = Place(blocks)
    me = at.z
    lanes = Lanes(send_sem, recv_sem)
    at.enter()
    every = blocks * own_rows
    if big:
        wo_rows = [(slice(y * half, (y + 1) * half), g_ref.at[0, y, :, :width]) for y in range(2)]
    else:
        wo_rows = [(slice(0, every), dgu_ref.at[0]), (slice(every, width), dgu_ref.at[1, :width - every])]
    wo_load = [pltpu.make_async_copy(wo_hbm.at[rows, :], place, load_sem.at[y])
               for y, (rows, place) in enumerate(wo_rows)]
    for load in wo_load:
        load.start()
    quarter = half // 4
    here = aligned(at.h * quarter, quarter)
    w_loads = [pltpu.make_async_copy(w_hbm.at[place], w_ref.at[place], load_sem.at[4 + i])
               for i, place in enumerate(((0,), (1, at.y), (1, at.oy, here)))]
    for load in w_loads:
        load.start()
    late = Shared(at, lanes, 4, None, functools.partial(weight_chunk, w_ref))
    if not big:
        cot_loads = [pltpu.make_async_copy(cot_hbm.at[b], cot_ref.at[b * own_rows:(b + 1) * own_rows, :],
                                           load_sem.at[7 + b]) for b in range(blocks)]
        for load in cot_loads:
            load.start()

    total_experts = experts * blocks
    srows = small_ref.shape[0]
    is_router = lax.broadcasted_iota(jnp.int32, (srows, width), 0) < total_experts
    router_ref[...] = jnp.zeros_like(router_ref)
    router_ref[:srows, :] = jnp.where(is_router, small_ref[...].astype(F32), 0.0).astype(BF16)
    gain_two = small_ref[total_experts + 1:total_experts + 2, :].astype(F32)

    mixes = lanes.slots(4)

    def mix_cols(head):
        return mix_ref.at[:, pl.ds(pl.multiple_of(head * qcols, HEAD), qcols)]

    for head in (at.xn, at.xs, at.sib):
        lanes.put(mixes + at.h, o_ref.at[aligned(head * own_rows, own_rows), :], mix_cols(at.h), head=head)
    mix_ref[:, pl.ds(pl.multiple_of(at.h * qcols, HEAD), qcols)] = o_ref[aligned(at.h * own_rows, own_rows), :]
    for head in (at.sib, at.xn, at.xs):
        lanes.arrived(mixes + head, mix_cols(head), head=head)
    for load in w_loads:
        load.wait()
    for k in (2, 3):
        late.scatter(k)
    for load in wo_load:
        load.wait()
    step = 512
    for i in range(width // step):
        cols = slice(i * step, (i + 1) * step)
        res_out[:, cols] = x_ref[:, cols].astype(F32) + sum(
            mm(mix_ref[:, rows], place[:, cols]) for rows, place in wo_rows)

    def inverse_two():
        res = res_out[...]
        return lax.rsqrt(jnp.mean(res * res, axis=-1, keepdims=True) + NORM_EPSILON)

    n2 = (res_out[...] * inverse_two() * gain_two).astype(BF16)
    chosen = chosen_ref[...] > 0.0
    logits = jnp.where(chosen, mm(n2, router_ref[...], NT), MASKED)
    e_top = jnp.where(chosen, jnp.exp(logits - jnp.max(logits, axis=-1, keepdims=True)), 0.0)
    gates = e_top / jnp.sum(e_top, axis=-1, keepdims=True)
    gates_ref[...] = gates
    own_x = xb_stage if big else xb_ref.at[me]
    own_x[:, :width] = n2
    own_x[:, width:] = split_lanes(gates)

    def move(src, dst):
        copy = pltpu.make_async_copy(src, dst, load_sem.at[3])
        copy.start()
        copy.wait()

    if big:
        move(xb_stage, xb_ref.at[me])
    xs_slot, xs_sent = lanes.slots(blocks), lanes.sends(blocks + 2)

    def xs_copy(b, to, send):
        return remote(xb_ref.at[b], xb_ref.at[b], send_sem.at[xs_sent + send], recv_sem.at[xs_slot + b], blk=to)

    pl.when(me > 0)(lambda: xs_copy(me, me - 1, blocks).start())
    pl.when(me < blocks - 1)(lambda: xs_copy(me, me + 1, blocks + 1).start())

    if big:
        def clear(i, _):
            for e in range(experts):
                for y in range(2):
                    g_ref[e, y, aligned(i * 64, 64), :] = jnp.zeros((64, g_ref.shape[3]), BF16)
            return 0

        lax.fori_loop(0, half // 64, clear, 0)
    else:
        for load in cot_loads:
            load.wait()
    for k in (2, 3):
        late.forward(k)
    for k in (2, 3):
        late.finish(k)
    back = ColumnSum(at, lanes, dx_ref, land_ref)
    lane = lax.broadcasted_iota(jnp.int32, (own_rows, LANES), 1)
    tile = 256

    def y_copy(b):
        return pltpu.make_async_copy(y_ref, y_out.at[b], y_sem)

    def block(b, first):
        if big:
            move(xb_ref.at[b], xb_stage)
            move(cot_hbm.at[b], cot_ref)
        x_in = xb_stage if big else xb_ref.at[b]
        band_all = slice(None) if big else aligned(b * own_rows, own_rows)
        lanes_all = pl.ds(pl.multiple_of(b * own_rows, own_rows), own_rows)
        acc_ref[...] = jnp.zeros_like(acc_ref)
        gg_ref[...] = jnp.zeros_like(gg_ref)

        def hidden(e, _):
            index = me * experts + e
            pack = x_in[:, width:].astype(F32)
            mine = (lane == index) | (lane == index + HALF_LANES)
            gate_ref[...] = jnp.sum(jnp.where(mine, pack, 0.0), axis=1, keepdims=True)

            def inner(t, total):
                low = pl.ds(pl.multiple_of(t * tile, tile), tile)
                high = pl.ds(pl.multiple_of(ffe + t * tile, tile), tile)
                out_cols = slice(width, width + half)
                gate_pre = mm(x_in[:, :half], w_ref[e, 0, :, low]) + mm(x_in[:, half:width], w_ref[e, 1, :, low])
                up = mm(x_in[:, :half], w_ref[e, 0, :, high]) + mm(x_in[:, half:width], w_ref[e, 1, :, high])
                back_h = (mm(cot_ref[band_all, :half], w_ref[e, 0, low, out_cols], NT)
                          + mm(cot_ref[band_all, half:], w_ref[e, 1, low, out_cols], NT))
                value, slope = gelu_parts(gate_pre)
                act = (value * up).astype(BF16).astype(F32)
                gate = gate_ref[...]
                ga_ref[e, :, low] = (gate * act).astype(BF16)
                if not big:
                    gat_ref[e, low, lanes_all] = (gate * act).T.astype(BF16)
                d_act = gate * back_h
                dgu_ref[e, band_all, low] = (d_act * up * slope).astype(BF16)
                dgu_ref[e, band_all, high] = (d_act * value).astype(BF16)
                return total + jnp.sum(act * back_h, axis=1, keepdims=True)

            total = lax.fori_loop(0, ffe // tile, inner, jnp.zeros((own_rows, 1), F32))
            gg_ref[...] += jnp.where(lane == index, total, 0.0)
            for y in range(2):
                acc_ref[:, y * half:(y + 1) * half] += mm(dgu_ref[e, band_all, :], w_ref[e, y, :, :width], NT)
            return 0

        lax.fori_loop(0, experts, hidden, 0)
        part = dx_stage if big else dx_ref.at[b]
        part[:, :width] = acc_ref[...].astype(BF16)
        part[:, width:] = split_lanes(gg_ref[...])
        if big:
            move(dx_stage, dx_ref.at[b])
        back.first_send(b)

        if big:
            xt_ref[...] = x_in[:, :width].astype(F32).T.astype(BF16)

            def weights(e, _):
                gat_ref[0] = ga_ref[e].astype(F32).T.astype(BF16)

                def rows(i, _):
                    band = aligned(i * tile, tile)
                    for y in range(2):
                        x_cols = xt_ref[aligned(y * half + i * tile, tile), :]
                        for n in range(width // step):
                            cols = slice(n * step, (n + 1) * step)
                            total = g_ref[e, y, band, cols].astype(F32) + mm(x_cols, dgu_ref[e, :, cols])
                            g_ref[e, y, band, cols] = total.astype(BF16)
                        out_cols = slice(width, width + half)
                        total = (g_ref[e, y, band, out_cols].astype(F32)
                                 + mm(gat_ref[0, band, :], cot_ref[:, y * half:(y + 1) * half]))
                        g_ref[e, y, band, out_cols] = total.astype(BF16)
                    return 0

                return lax.fori_loop(0, half // tile, rows, 0)

            lax.fori_loop(0, experts, weights, 0)
        else:
            xt_ref[:, lanes_all] = x_in[:, :width].astype(F32).T.astype(BF16)

        pl.when(jnp.logical_not(first))(lambda: y_copy(b).wait())
        for y in range(2):
            total = mm(ga_ref[0], w_ref[0, y, :, width:])
            for e in range(1, experts):
                total = total + mm(ga_ref[e], w_ref[e, y, :, width:])
            y_ref[:, y * half:(y + 1) * half] = total.astype(BF16)
        y_copy(b).start()

    def distance(d, _):
        for b, origin, to in ((me - d, me - 1, me + 1), (me + d, me + 1, me - 1)):
            @pl.when((d > 0) & (b >= 0) & (b < blocks))
            def _(b=b, origin=origin, to=to):
                xs_copy(b, origin, 0).wait_recv()
                pl.when((to >= 0) & (to < blocks))(lambda: xs_copy(b, to, b).start())

        def side(s, _):
            b = jnp.where(s == 0, me - d, me + d)

            @pl.when((b >= 0) & (b < blocks) & ((d > 0) | (s == 0)))
            def _():
                block(jnp.clip(b, 0, blocks - 1), d == 0)

            return 0

        return lax.fori_loop(0, 2, side, 0)

    lax.fori_loop(0, blocks, distance, 0)
    y_copy(me).wait()

    late.settle()
    total_ref = g_ref if big else w_ref

    def weights_of(e):
        def rows(i, _):
            cols = pl.ds(pl.multiple_of(i * tile, tile), tile)
            for y in range(2):
                total = mm(xt_ref[y * half:(y + 1) * half, :], dgu_ref[e, :, cols])
                total_ref[e, y, :, cols] = total.astype(BF16)
            return 0

        def outs(i, _):
            for y in range(2):
                cols = pl.ds(pl.multiple_of(y * half + i * tile, tile), tile)
                place = pl.ds(pl.multiple_of(width + i * tile, tile), tile)
                total_ref[e, y, :, place] = mm(gat_ref[e], cot_ref[:, cols]).astype(BF16)
            return 0

        lax.fori_loop(0, 2 * ffe // tile, rows, 0)
        lax.fori_loop(0, half // tile, outs, 0)

    chunks = 4
    piece = half // chunks
    cores = lanes.slots(chunks)
    if not big:
        weights_of(1 - at.c)
    for k in range(chunks):
        band = pl.ds(k * piece, piece)
        lanes.put(cores + k, total_ref.at[1 - at.c, :, band, :], core_land.at[:, band, :], head=at.sib)

    def add(b, rows):
        if big:
            move(dx_ref.at[b, rows, :], dx_stage.at[rows, :])
            move(land_ref.at[b, rows, :], land_stage.at[rows, :])
            dx_stage[rows, :] = (dx_stage[rows, :].astype(F32) + land_stage[rows, :].astype(F32)).astype(BF16)
            move(dx_stage.at[rows, :], dx_ref.at[b, rows, :])
        else:
            dx_ref[b, rows, :] = (dx_ref[b, rows, :].astype(F32) + land_ref[b, rows, :].astype(F32)).astype(BF16)

    def core_sum(k):
        band = pl.ds(k * piece, piece)
        lanes.arrived(cores + k, core_land.at[:, band, :], head=at.sib)
        move(core_land.at[:, band, :], stage_ref)
        for y in range(2):
            total = total_ref[at.c, y, band, :].astype(F32) + stage_ref[y].astype(F32)
            total_ref[at.c, y, band, :] = total.astype(BF16)

    for phase in range(2):
        for d in range(1, blocks):
            back.relay(phase, d, add)
    if not big:
        weights_of(at.c)
    for k in range(chunks):
        core_sum(k)
    keep = pltpu.make_async_copy(total_ref.at[at.c], sums_out, load_sem.at[0])
    keep.start()

    if big:
        move(dx_ref.at[me], dx_stage)
    own_part = dx_stage if big else dx_ref.at[me]
    acc_ref[...] = own_part[:, :width].astype(F32)
    gg_ref[...] = own_part[:, width:].astype(F32)

    def take(slot):
        if big:
            move(land_ref.at[slot], land_stage)
        came = land_stage if big else land_ref.at[slot]
        acc_ref[...] += came[:, :width].astype(F32)
        gg_ref[...] += came[:, width:].astype(F32)

    for side in range(2):
        back.arrive(side, take)
    both = gg_ref[...]
    gate_grads = jnp.where(lane < HALF_LANES, both + pltpu.roll(both, HALF_LANES, 1), 0.0)
    gates = gates_ref[...]
    d_logits = (gates * (gate_grads - jnp.sum(gates * gate_grads, axis=-1, keepdims=True))).astype(BF16)
    inv = inverse_two()
    hat = res_out[...] * inv
    n2 = (hat * gain_two).astype(BF16)
    small_out[...] = mm(d_logits.astype(F32).T.astype(BF16), n2)[:small_out.shape[0], :]
    d_n2 = acc_ref[...] + mm(d_logits, router_ref[...])
    small_out[total_experts + 1:total_experts + 2, :] = jnp.sum(d_n2 * hat, axis=0, keepdims=True)
    pulled = d_n2 * gain_two
    if big:
        move(cot_hbm.at[me], cot_ref)
    own_cot = cot_ref[...] if big else cot_ref[aligned(me * own_rows, own_rows), :]
    grad = own_cot.astype(F32) + inv * (pulled - hat * jnp.mean(pulled * hat, axis=-1, keepdims=True))
    grad_out[...] = grad
    attn_out[...] = grad.astype(BF16)
    keep.wait()
    for b in range(blocks):
        up, down = (b < me) & (me < blocks - 1), (b > me) & (me > 0)
        pl.when(up)(lambda b=b: xs_copy(b, me + 1, b).wait_send())
        pl.when(down)(lambda b=b: xs_copy(b, me - 1, b).wait_send())
    pl.when(me > 0)(lambda: xs_copy(me, me - 1, blocks).wait_send())
    pl.when(me < blocks - 1)(lambda: xs_copy(me, me + 1, blocks + 1).wait_send())
    back.finish()
    lanes.drain()


def expert_layer(o, x, small, chosen, wo, w, cot):
    own_rows, width = x.shape
    blocks = cot.shape[0]
    experts, _, half, wide = w.shape
    ffe = half
    pack = width + LANES
    big = blocks > 4
    kept = own_rows if big else blocks * own_rows
    vm = pl.BlockSpec(memory_space=pltpu.VMEM)
    hbm = pl.BlockSpec(memory_space=pl.ANY)
    sds = jax.ShapeDtypeStruct
    column = [((blocks, own_rows, pack), BF16), ((blocks, own_rows, pack), BF16), ((blocks + 1, own_rows, pack), BF16)]
    if big:
        extra_out, extra_spec = tuple(sds(*c) for c in column), [hbm] * 3
        extra_scratch = [pltpu.VMEM((own_rows, pack), BF16)] * 3 + [pltpu.VMEM(w.shape, BF16)]
    else:
        extra_out, extra_spec = (), []
        extra_scratch = [pltpu.VMEM(*c) for c in column]
    outs = pl.pallas_call(
        expert_kernel,
        out_shape=(
            sds((own_rows, width), F32),
            sds((own_rows, width), F32),
            sds((own_rows, width), BF16),
            sds((-(-(experts * blocks + 2) // 8) * 8, width), F32),
            sds((2, half, wide), BF16),
            sds((blocks, own_rows, width), BF16),
            sds((2, half, wide), BF16),
        ) + extra_out,
        in_specs=[vm] * 4 + [hbm] * 3,
        out_specs=[vm] * 4 + [hbm] * 3 + extra_spec,
        scratch_shapes=extra_scratch + [
            pltpu.VMEM((own_rows, width), BF16),
            pltpu.VMEM(w.shape, BF16),
            pltpu.VMEM((kept, width), BF16),
            pltpu.VMEM((own_rows, width), F32),
            pltpu.VMEM((own_rows, 1), F32),
            pltpu.VMEM((experts, kept, 2 * ffe), BF16),
            pltpu.VMEM((experts, own_rows, ffe), BF16),
            pltpu.VMEM((width, kept), BF16),
            pltpu.VMEM((experts, ffe, kept), BF16),
            pltpu.VMEM((own_rows, LANES), F32),
            pltpu.VMEM((own_rows, width), BF16),
            pltpu.VMEM((2, half // 4, wide), BF16),
            pltpu.VMEM((own_rows, LANES), F32),
            pltpu.VMEM((LANES, width), BF16),
            pltpu.SemaphoreType.DMA((7 + blocks,)),
            pltpu.SemaphoreType.DMA,
        ] + semaphores(blocks),
        compiler_params=pltpu.CompilerParams(
            vmem_limit_bytes=VMEM_BYTES, collective_id=1, has_side_effects=True),
    )(o, x, small, chosen, wo, w, cot)
    return outs[:6]


class ExpertSums:
    CHUNKS = 8

    def __init__(self, at, lanes, grads, own, land_y, land_x, out, load_sem, keep_sem):
        self.at, self.lanes = at, lanes
        self.grads, self.own, self.out = grads, own, out
        self.land_y, self.land_x = land_y, land_x
        self.load_sem, self.keep_sem = load_sem, keep_sem
        self.rows = grads.shape[1] // self.CHUNKS
        n = self.CHUNKS
        self.ys, self.xr, self.cg = [lanes.slots(n) for _ in range(3)]
        self.sent = []
        self.kept = []

    def chunk(self, k):
        return pl.ds(k * self.rows, self.rows)

    def load(self):
        self.loads = [pltpu.make_async_copy(self.grads.at[y], self.own.at[y], self.load_sem.at[i])
                      for i, y in enumerate((self.at.oy, self.at.y))]
        for copy in self.loads:
            copy.start()

    def to_y(self):
        self.loads[0].wait()
        for k in range(self.CHUNKS):
            rows = self.chunk(k)
            self.sent.append(self.lanes.put(
                self.ys + k, self.own.at[self.at.oy, rows, :], self.land_y.at[rows, :], fsdp=self.at.oy))

    def y_sent(self):
        for copy in self.sent:
            self.lanes.settle(copy)

    def to_x(self, k):
        at, rows = self.at, self.chunk(k)
        if k == 0:
            self.loads[1].wait()
        self.lanes.arrived(self.ys + k, self.land_y.at[rows, :], fsdp=at.oy)
        total = self.own[at.y, rows, :].astype(F32) + self.land_y[rows, :].astype(F32)
        self.own[at.y, rows, :] = total.astype(BF16)
        self.lanes.put(self.xr + k, self.own.at[at.y, rows, :], self.land_x.at[rows, :], head=at.xn)

    def share(self, k):
        at, rows = self.at, self.chunk(k)
        self.lanes.arrived(self.xr + k, self.land_x.at[rows, :], head=at.xn)
        total = self.own[at.y, rows, :].astype(F32) + self.land_x[rows, :].astype(F32)
        self.land_x[rows, :] = total.astype(BF16)
        done, place = self.land_x.at[rows, :], self.out.at[at.c, rows, :]
        self.lanes.put(self.cg + k, done, place, head=at.sib)
        keep = pltpu.make_async_copy(done, place, self.keep_sem.at[k])
        keep.start()
        self.kept.append(keep)

    def finish(self):
        at = self.at
        for k in range(self.CHUNKS):
            self.lanes.arrived(self.cg + k, self.out.at[1 - at.c, self.chunk(k), :], head=at.sib)
            self.kept[k].wait()


class OutputSums:
    PARTS = 4

    def __init__(self, at, lanes, grad, land_y, land_z, out):
        self.at, self.lanes, self.grad = at, lanes, grad
        self.land_y, self.land_z, self.out = land_y, land_z, out
        self.rows = grad.shape[0] // self.PARTS
        self.ys = lanes.slots()
        self.zr, self.zg = lanes.slots(at.blocks), lanes.slots(self.PARTS)
        self.xg, self.cg = lanes.slots(self.PARTS), lanes.slots(self.PARTS)
        self.owner, self.giver = at.y == at.x, at.y != at.x
        self.summer = at.z < self.PARTS
        self.part = at.z % self.PARTS
        self.mine = aligned(self.part * self.rows, self.rows)

    def to_z(self):
        at = self.at
        for p in range(self.PARTS):
            self.lanes.put(self.zr + at.z, self.grad.at[pl.ds(p * self.rows, self.rows), :], self.land_z.at[at.z],
                           when=at.z != p, blk=p)

    def to_y(self, fetch):
        at = self.at
        for z in at.others():
            self.lanes.arrived(self.zr + z, self.land_z.at[z], when=self.summer, blk=z)

        @pl.when(self.summer)
        def _():
            total = self.grad[self.mine, :].astype(F32)
            for z in at.others():
                total = total + fetch(self.land_z.at[z])[...].astype(F32)
            self.grad[self.mine, :] = total.astype(BF16)

        self.lanes.put(self.ys, self.grad.at[self.mine, :], self.land_y, when=self.summer & self.giver, fsdp=at.oy)

    def place(self, core, p):
        return self.out.at[aligned(core * self.PARTS * self.rows + p * self.rows, self.rows), :]

    def share(self):
        at, p = self.at, self.part
        ready = self.summer & self.owner
        self.lanes.arrived(self.ys, self.land_y, when=ready, fsdp=at.oy)
        at_rows = aligned(at.c * self.PARTS * self.rows + p * self.rows, self.rows)

        @pl.when(ready)
        def _():
            total = self.grad[self.mine, :].astype(F32) + self.land_y[...].astype(F32)
            self.out[at_rows, :] = total.astype(BF16)

        place = self.place(at.c, p)
        for z in at.others():
            self.lanes.put(self.zg + p, place, place, when=ready, blk=z)
        self.lanes.put(self.xg + p, place, place, when=ready, head=at.xn)
        self.lanes.put(self.cg + p, place, place, when=ready, head=at.sib)

    def pass_on(self):
        at = self.at
        for p in range(self.PARTS):
            place = self.place(at.c, p)
            later = self.owner & (at.z != p)
            self.lanes.arrived(self.zg + p, place, when=later, blk=p)
            self.lanes.put(self.xg + p, place, place, when=later, head=at.xn)
            self.lanes.put(self.cg + p, place, place, when=later, head=at.sib)

    def take_over(self):
        at = self.at
        for p in range(self.PARTS):
            place = self.place(at.c, p)
            self.lanes.arrived(self.xg + p, place, when=self.giver, head=at.xn)
            self.lanes.put(self.cg + p, place, place, when=self.giver, head=at.sib)

    def finish(self):
        at = self.at
        for p in range(self.PARTS):
            self.lanes.arrived(self.cg + p, self.place(1 - at.c, p), head=at.sib)


def back_kernel(attn_ref, q_ref, ot_ref, start_ref, lse_ref, x_ref, cos_ref, sin_ref, gain_ref, small_ref,
                kv_in, wo_hbm, grads_hbm, y_in, res_hbm, res_grad_hbm, n1_hbm, w_hbm,
                block_out, tokens_out, small_out, kv_out, experts_out, output_out, query_out, y_land, *rest):
    blocks = kv_in.shape[0]
    big = blocks > 4
    dkv_stage = dwo_stage = None
    if big:
        yp_ref, dkv_land, dkv_sib, dwo_z, kv_ref, dkv_stage, dwo_stage, y_stage, kv_stage, *rest = rest
    else:
        yp_ref, dkv_land, dkv_sib, dwo_z, kv_ref, *rest = rest
    (dq_ref, dk_ref, dv_ref, kt_ref, delta_ref, do_ref, ag_ref, wo_ref, dwo_ref, dwo_y, dwo_land,
     own_ref, ey_ref, ex_ref, acc_ref, y_other, w_ref, dpre_ref, dn_sib, dn_x, dw_ref, dw_y, dw_z,
     sm_ref, sm_a, sm_b, sm_y, sm_z, land_ref, dkv_ref, load_sem, keep_sem, send_sem, recv_sem) = rest
    heads, rows, _ = q_ref.shape
    own_rows, width = attn_ref.shape
    half = width // 2
    half_rows = rows // 2
    qcols = heads * HEAD
    gain_row = 2 * blocks
    at = Place(blocks)
    me = at.z
    lanes = Lanes(send_sem, recv_sem)
    at.enter()
    experts = ExpertSums(at, lanes, grads_hbm, own_ref, ey_ref, ex_ref, experts_out, load_sem, keep_sem)
    output = OutputSums(at, lanes, dwo_ref, dwo_y, dwo_z, dwo_land)
    sums = ColumnSum(at, lanes, yp_ref, y_land)
    experts.load()
    forward, near, far, passed = gather_heads(at, lanes, attn_ref, ag_ref)

    def load(src, dst, sem):
        copy = pltpu.make_async_copy(src, dst, load_sem.at[sem])
        copy.start()
        return copy

    def move(src, dst):
        load(src, dst, 5).wait()

    wo_load = load(wo_hbm.at[aligned(at.h * qcols, qcols), :], wo_ref, 2)
    y_load = load(y_in, yp_ref, 3)
    if not big:
        kv_load = load(kv_in, kv_ref, 4)
    experts.to_y()
    y_load.wait()
    for b in range(blocks):
        sums.first_send(b)

    def add(b, band):
        move(y_land.at[b, band, :], y_other.at[band, :])
        if big:
            move(yp_ref.at[b, band, :], y_stage.at[band, :])
            y_stage[band, :] = (y_stage[band, :].astype(F32) + y_other[band, :].astype(F32)).astype(BF16)
            move(y_stage.at[band, :], yp_ref.at[b, band, :])
        else:
            yp_ref[b, band, :] = (yp_ref[b, band, :].astype(F32) + y_other[band, :].astype(F32)).astype(BF16)

    def fetch(stage):
        def get(ref):
            if big:
                move(ref, stage)
                return stage
            return ref
        return get

    wo_load.wait()

    def mix_back(head):
        band = aligned(head * own_rows, own_rows)
        grad = mm(ag_ref[band, :], wo_ref[...], NT).astype(BF16)
        for hh in range(heads):
            do_ref[hh, band, :] = grad[:, hh * HEAD:(hh + 1) * HEAD]

    ag_ref[aligned(at.h * own_rows, own_rows), :] = attn_ref[...]
    mix_back(at.h)
    near()
    mix_back(at.sib)
    forward()
    mix_back(at.xn)
    far()
    mix_back(at.xs)
    step = 512

    def weight_back(i, _):
        cols = pl.ds(pl.multiple_of(i * step, step), step)
        dwo_ref[:, cols] = mm(ot_ref[...], ag_ref[:, cols]).astype(BF16)
        return 0

    lax.fori_loop(0, width // step, weight_back, 0)
    output.to_z()
    lanes.settle(passed[0])
    n1_load = load(n1_hbm, ag_ref, 2)
    w_load = load(w_hbm, w_ref, 3)
    dq_ref[...] = jnp.zeros_like(dq_ref)
    for hh in range(heads):
        prod = do_ref[hh].astype(F32).T * ot_ref[hh * HEAD:(hh + 1) * HEAD, :].astype(F32)
        delta_ref[hh] = jnp.sum(prod, axis=0, keepdims=True)
    if not big:
        kv_load.wait()

    for k in (0, 1):
        experts.to_x(k)
    beside = [[(experts.to_x, 2), (experts.share, 0)],
              [(experts.to_x, 3), (experts.share, 1), (experts.to_x, 4)],
              [(experts.to_x, 5), (experts.share, 2), (experts.share, 3)]]

    def advance():
        for f, k in (beside.pop(0) if beside else ()):
            f(k)

    def opening(b):
        if big:
            move(kv_in.at[b], kv_stage)
        kv = kv_stage if big else kv_ref.at[b]
        kt_ref[...] = kv[:, :HEAD].astype(F32).T.astype(BF16)
        dk_ref[...] = jnp.zeros_like(dk_ref)
        dv_ref[...] = jnp.zeros_like(dv_ref)
        return kv

    def closing(b, kv):
        kv[:, :HEAD] = (dk_ref[...] * SCORE_SCALE).astype(BF16)
        kv[:, HEAD:] = dv_ref[...].astype(BF16)
        if big:
            move(kv_stage, kv_ref.at[b])

    def block(b):
        kv = opening(b)

        def tile(t, _):
            hh, i = t // (rows // TILE), t % (rows // TILE)
            cols = pl.ds(pl.multiple_of(i * TILE, TILE), TILE)
            unattend_tile(hh, cols, kv[:, :HEAD], kv[:, HEAD:], kt_ref[...], q_ref, do_ref,
                          start_ref, lse_ref, delta_ref, dq_ref, dk_ref, dv_ref, b * rows, None)
            return 0

        lax.fori_loop(0, heads * (rows // TILE), tile, 0)
        closing(b, kv)

    def half_of(core):
        return aligned(core * half_rows, half_rows)

    mine, other = half_of(at.c), half_of(1 - at.c)
    pair, column = lanes.slots(blocks), lanes.slots(blocks)

    def to_sibling(b, when):
        lanes.put(pair + b, kv_ref.at[b, other, :], dkv_sib.at[b], when=when, head=at.sib)

    def to_column(b):
        lanes.arrived(pair + b, dkv_sib.at[b], when=b < me, head=at.sib)

        @pl.when(b < me)
        def _():
            came = fetch(dkv_stage)(dkv_sib.at[b])
            if big:
                move(kv_ref.at[b, mine, :], kv_stage.at[mine, :])
            kv = kv_stage if big else kv_ref.at[b]
            kv[mine, :] = (kv[mine, :].astype(F32) + came[...].astype(F32)).astype(BF16)
            if big:
                move(kv_stage.at[mine, :], kv_ref.at[b, mine, :])

        lanes.put(column + me, kv_ref.at[b, mine, :], dkv_land.at[me], when=b < me, blk=b)

    for b in range(blocks - 1):
        pl.when(b < me)(functools.partial(block, b))
        to_sibling(b, b < me)
        sums.relay(0, b + 1, add)
        advance()
        if b > 0:
            to_column(b - 1)
    while beside:
        advance()
    to_column(blocks - 2)

    kv_own = opening(me)
    for i in range(rows // TILE):
        n = (i + 1) * TILE

        def diagonal(hh, _, i=i, n=n):
            unattend_tile(hh, slice(i * TILE, n), kv_own[:n, :HEAD], kv_own[:n, HEAD:], kt_ref[:, :n], q_ref, do_ref,
                          start_ref, lse_ref, delta_ref, dq_ref, dk_ref, dv_ref,
                          me * rows, me * rows + i * TILE)
            return 0

        lax.fori_loop(0, heads, diagonal, 0)
    closing(me, kv_own)
    to_sibling(me, None)
    for d in range(1, blocks):
        sums.relay(1, d, add)

    def unrotate(u, band):
        return u * cos_ref[band, :] - pltpu.roll(u, HEAD // 2, 1) * sin_ref[band, :]

    for hh in range(heads):
        dpre_ref[:, hh * HEAD:(hh + 1) * HEAD] = unrotate((dq_ref[hh] * SCORE_SCALE).T, slice(None)).astype(BF16)
    n1_load.wait()
    w_load.wait()
    n1_ref = ag_ref
    parts = 4
    part = half // parts
    band_rows = 256
    query_cols, keyval_cols = slice(0, qcols), slice(qcols, qcols + 2 * HEAD)

    def weight_half(y, cols_out):
        def body(i, _):
            cols = pl.ds(pl.multiple_of(y * half + i * band_rows, band_rows), band_rows)
            dw_ref[aligned(y * half + i * band_rows, band_rows), cols_out] = (
                mm(n1_ref[:, cols], dpre_ref[:, cols_out], TN).astype(BF16))
            return 0

        lax.fori_loop(0, half // band_rows, body, 0)

    def weight_part(y, p):
        return aligned(y * half + p * part, part)

    ys = (lanes.slots(parts), lanes.slots(parts))

    def weight_to_y(i, cols_out):
        weight_half(at.oy, cols_out)
        for p in range(parts):
            lanes.put(ys[i] + p, dw_ref.at[weight_part(at.oy, p), cols_out],
                      dw_y.at[pl.ds(p * part, part), cols_out], fsdp=at.oy)

    weight_to_y(0, query_cols)
    experts.to_x(6)

    dpre_ref[other, qcols:] = jnp.zeros((half_rows, 2 * HEAD), BF16)
    dkv_ref[:, :HEAD] = dk_ref[mine, :] * SCORE_SCALE
    dkv_ref[:, HEAD:] = dv_ref[mine, :]
    lanes.arrived(pair + me, dkv_sib.at[me], head=at.sib)
    dkv_ref[...] += fetch(dkv_stage)(dkv_sib.at[me])[...].astype(F32)
    for z in range(1, blocks):
        @pl.when(me < z)
        def _(z=z):
            lanes.arrived(column + z, dkv_land.at[z], blk=z)
            dkv_ref[...] += fetch(dkv_stage)(dkv_land.at[z])[...].astype(F32)

    dpre_ref[mine, qcols:qcols + HEAD] = unrotate(dkv_ref[:, :HEAD], mine).astype(BF16)
    dpre_ref[mine, qcols + HEAD:] = dkv_ref[:, HEAD:].astype(BF16)
    weight_to_y(1, keyval_cols)

    def input_part(head):
        return mm(dpre_ref[aligned(head * own_rows, own_rows), :], w_ref[...], NT)

    experts.y_sent()

    def dn_ref(i):
        return own_ref.at[at.oy, i * own_rows:(i + 1) * own_rows, :width]

    relay, direct, across = lanes.slots(), lanes.slots(), lanes.slots()
    dn_ref(0)[...] = input_part(at.xs).astype(BF16)
    lanes.put(relay, dn_ref(0), dn_sib.at[0], head=at.sib)
    dn_ref(2)[...] = input_part(at.sib).astype(BF16)
    lanes.put(direct, dn_ref(2), dn_sib.at[1], head=at.sib)
    lanes.arrived(relay, dn_sib.at[0], head=at.sib)
    dn_ref(1)[...] = (input_part(at.xn) + dn_sib[0].astype(F32)).astype(BF16)
    lanes.put(across, dn_ref(1), dn_x, head=at.xn)
    experts.to_x(7)
    experts.share(4)
    weight_half(at.y, slice(None))
    output.to_y(fetch(dwo_stage))

    zr = lanes.slots(blocks)
    for p in range(parts):
        rows_p = weight_part(at.y, p)
        for i, cols_out in enumerate((query_cols, keyval_cols)):
            lanes.arrived(ys[i] + p, dw_y.at[pl.ds(p * part, part), cols_out], fsdp=at.oy)
        total = dw_ref[rows_p, :].astype(F32) + dw_y[pl.ds(p * part, part), :].astype(F32)
        dw_ref[rows_p, :] = total.astype(BF16)
        lanes.put(zr + at.z, dw_ref.at[rows_p, :], dw_z.at[at.z], when=at.z != p, blk=p)
    experts.share(5)
    output.share()

    move(res_hbm, acc_ref)
    if big:
        move(yp_ref.at[me], y_stage)
    acc_ref[...] += (y_stage if big else yp_ref.at[me])[...].astype(F32)

    def take(slot):
        move(y_land.at[slot], y_other)
        acc_ref[...] += y_other[...].astype(F32)

    for side in range(2):
        sums.arrive(side, take)
    block_out[...] = acc_ref[...].astype(BF16)

    res_load = load(res_grad_hbm, acc_ref, 5)
    own = input_part(at.h)
    lanes.arrived(direct, dn_sib.at[1], head=at.sib)
    own = own + dn_sib[1].astype(F32)
    lanes.arrived(across, dn_x, head=at.xn)
    own = own + dn_x[...].astype(F32)
    x = x_ref[...].astype(F32)
    inv = lax.rsqrt(jnp.mean(x * x, axis=-1, keepdims=True) + NORM_EPSILON)
    hat = x * inv
    pulled = own * gain_ref[gain_row:gain_row + 1, :].astype(F32)
    slope = inv * (pulled - hat * jnp.mean(pulled * hat, axis=-1, keepdims=True))
    res_load.wait()
    tokens_out[...] = (acc_ref[...] + slope).astype(BF16)
    sm_ref[...] = small_ref[...]
    sm_ref[gain_row:gain_row + 1, :] = jnp.sum(own * hat, axis=0, keepdims=True)
    sa, sb, sy, sz = lanes.slots(), lanes.slots(), lanes.slots(), lanes.slots(blocks)
    lanes.put(sa, sm_ref, sm_a, head=at.sib)
    experts.share(6)

    p = at.z % parts
    summer = at.z < parts
    zg, xg, cg, cf = lanes.slots(parts), lanes.slots(parts), lanes.slots(parts), lanes.slots(parts)

    def place(head, q):
        return land_ref.at[head, pl.ds(q * part, part), :]

    for z in at.others():
        lanes.arrived(zr + z, dw_z.at[z], when=summer, blk=z)
    mine_w = weight_part(at.y, p)

    @pl.when(summer)
    def _():
        total = dw_ref[mine_w, :].astype(F32)
        for z in at.others():
            total = total + dw_z[z].astype(F32)
        dw_ref[mine_w, :] = total.astype(BF16)
        land_ref[at.h, aligned(p * part, part), :] = total.astype(BF16)

    for z in at.others():
        lanes.put(zg + p, dw_ref.at[mine_w, :], place(at.h, p), when=summer, blk=z)
    lanes.put(xg + p, dw_ref.at[mine_w, :], place(at.h, p), when=summer, head=at.xn)
    lanes.put(cg + p, dw_ref.at[mine_w, :], place(at.h, p), when=summer, head=at.sib)
    lanes.arrived(sa, sm_a, head=at.sib)
    sm_a[...] = sm_a[...] + sm_ref[...]
    lanes.put(sb, sm_a, sm_b, head=at.xn)
    output.pass_on()
    experts.share(7)

    lanes.arrived(sb, sm_b, head=at.xn)
    sm_b[...] = sm_a[...] + sm_b[...]
    mine_cols = pl.ds(pl.multiple_of(at.y * half, half), half)
    other_cols = pl.ds(pl.multiple_of(at.oy * half, half), half)
    lanes.put(sy, sm_b.at[:, other_cols], sm_y, fsdp=at.oy)
    for q in range(parts):
        later = at.z != q
        lanes.arrived(zg + q, place(at.h, q), when=later, blk=q)
        lanes.put(xg + q, place(at.h, q), place(at.h, q), when=later, head=at.xn)
        lanes.put(cg + q, place(at.h, q), place(at.h, q), when=later, head=at.sib)
    lanes.arrived(sy, sm_y, fsdp=at.oy)
    sm_z[at.z] = sm_b[:, mine_cols] + sm_y[...]
    for z in at.others():
        lanes.put(sz + at.z, sm_z.at[at.z], sm_z.at[at.z], blk=z)
    output.take_over()
    for q in range(parts):
        lanes.arrived(xg + q, place(at.xn, q), head=at.xn)
        lanes.put(cf + q, place(at.xn, q), place(at.xn, q), head=at.sib)
    for z in at.others():
        lanes.arrived(sz + z, sm_z.at[z], blk=z)
    total = sm_z[0]
    for z in range(1, blocks):
        total = total + sm_z[z]
    small_out[...] = total
    output.finish()
    keeps = [load(dwo_land, output_out, 0)]
    for q in range(parts):
        lanes.arrived(cg + q, place(at.sib, q), head=at.sib)
        lanes.arrived(cf + q, place(at.xs, q), head=at.sib)
    for head in range(4):
        keeps.append(load(land_ref.at[head, :, :qcols], query_out.at[:, head * qcols:(head + 1) * qcols], 1 + head))
    for g in range(KEYVALUE_HEADS):
        both = land_ref[2 * g, :, qcols:].astype(F32) + land_ref[2 * g + 1, :, qcols:].astype(F32)
        kv_out[:, g * HEAD:(g + 1) * HEAD] = both[:, :HEAD]
        kv_out[:, (KEYVALUE_HEADS + g) * HEAD:(KEYVALUE_HEADS + g + 1) * HEAD] = both[:, HEAD:]
    experts.finish()
    for keep in keeps:
        keep.wait()
    sums.finish()
    lanes.drain()


def backward(attn_grad, q, ot, start, lse, x, cosine, sine, gain, small, kv, wo, grads, y_parts, res, res_grad, n1, w):
    heads, rows, _ = q.shape
    blocks = kv.shape[0]
    own_rows, width = attn_grad.shape
    qcols = heads * HEAD
    _, half, wide = grads.shape
    cols = w.shape[1]
    srows = small.shape[0]
    n = ExpertSums.CHUNKS
    vm = pl.BlockSpec(memory_space=pltpu.VMEM)
    hbm = pl.BlockSpec(memory_space=pl.ANY)
    part = qcols // OutputSums.PARTS
    sds = jax.ShapeDtypeStruct
    column = [((blocks, own_rows, width), BF16), ((blocks, rows // 2, 2 * HEAD), BF16),
              ((blocks, rows // 2, 2 * HEAD), BF16), ((blocks, part, width), BF16), (kv.shape, BF16)]
    if blocks > 4:
        extra_out, extra_spec = tuple(sds(*c) for c in column), [hbm] * 5
        extra_scratch = [pltpu.VMEM((rows // 2, 2 * HEAD), BF16), pltpu.VMEM((part, width), BF16),
                         pltpu.VMEM((own_rows, width), BF16), pltpu.VMEM((rows, 2 * HEAD), BF16)]
    else:
        extra_out, extra_spec = (), []
        extra_scratch = [pltpu.VMEM(*c) for c in column]
    return pl.pallas_call(
        back_kernel,
        out_shape=(
            sds((own_rows, width), BF16),
            sds((own_rows, width), BF16),
            sds((srows, half), F32),
            sds((half, 2 * KEYVALUE_HEADS * HEAD), F32),
            sds((2, half, wide), BF16),
            sds((2 * qcols, width), BF16),
            sds((half, rows // own_rows * qcols), BF16),
            sds((blocks + 1, own_rows, width), BF16),
        ) + extra_out,
        in_specs=[vm] * 10 + [hbm] * 8,
        out_specs=[vm] * 4 + [hbm] * 4 + extra_spec,
        scratch_shapes=extra_scratch + [
            pltpu.VMEM((heads, HEAD, rows), F32),
            pltpu.VMEM((rows, HEAD), F32),
            pltpu.VMEM((rows, HEAD), F32),
            pltpu.VMEM((HEAD, rows), BF16),
            pltpu.VMEM((heads, 1, rows), F32),
            pltpu.VMEM((heads, rows, HEAD), BF16),
            pltpu.VMEM((rows, width), BF16),
            pltpu.VMEM((qcols, width), BF16),
            pltpu.VMEM((qcols, width), BF16),
            pltpu.VMEM((part, width), BF16),
            pltpu.VMEM((2 * qcols, width), BF16),
            pltpu.VMEM((2, half, wide), BF16),
            pltpu.VMEM((half, wide), BF16),
            pltpu.VMEM((half, wide), BF16),
            pltpu.VMEM((own_rows, width), F32),
            pltpu.VMEM((own_rows, width), BF16),
            pltpu.VMEM((width, cols), BF16),
            pltpu.VMEM((rows, cols), BF16),
            pltpu.VMEM((2, own_rows, width), BF16),
            pltpu.VMEM((own_rows, width), BF16),
            pltpu.VMEM((width, cols), BF16),
            pltpu.VMEM((half, cols), BF16),
            pltpu.VMEM((blocks, half // 4, cols), BF16),
            pltpu.VMEM((srows, width), F32),
            pltpu.VMEM((srows, width), F32),
            pltpu.VMEM((srows, width), F32),
            pltpu.VMEM((srows, half), F32),
            pltpu.VMEM((blocks, srows, half), F32),
            pltpu.VMEM((rows // own_rows, half, cols), BF16),
            pltpu.VMEM((rows // 2, 2 * HEAD), F32),
            pltpu.SemaphoreType.DMA((6,)),
            pltpu.SemaphoreType.DMA((n,)),
        ] + semaphores(blocks),
        compiler_params=pltpu.CompilerParams(
            vmem_limit_bytes=VMEM_BYTES, collective_id=2, has_side_effects=True),
    )(attn_grad, q, ot, start, lse, x, cosine, sine, gain, small, kv, wo, grads, y_parts, res, res_grad, n1, w)[:7]


def on_device(tokens, documents, routes, cotangent, first_gain, query_weight, keyvalue_weight, output_weight,
              second_gain, router_weight, expert_in, expert_out):
    z = lax.axis_index("blk")
    blocks = lax.axis_size("blk")
    rows, width = tokens.shape[1:]
    group = lax.axis_size("head") * rows
    experts = router_weight.shape[1]
    half = query_weight.shape[0]

    small_rows = -(-(2 + experts) // 16) * 16
    small = jnp.concatenate([router_weight.T, first_gain[None], second_gain[None],
                             jnp.zeros((small_rows - 2 - experts, half), BF16)], axis=0)
    pos = (z * group + jnp.arange(group, dtype=jnp.int32)).astype(F32)
    inverse = jnp.power(ROPE_BASE, -jnp.arange(HEAD // 2).astype(F32) * 2.0 / HEAD)
    angle = pos[:, None] * inverse[None, :]
    cos, sin = jnp.cos(angle), jnp.sin(angle)
    cosine = jnp.concatenate([cos, cos], axis=-1)
    sine = jnp.concatenate([-sin, sin], axis=-1)
    doc = documents[0]
    doc_q = lax.dynamic_slice_in_dim(doc, z * group, group, 0)
    start = sum(jnp.where(doc_q > d, jnp.sum((doc == d).astype(jnp.int32)), 0) for d in range(DOCUMENTS - 1))[None, :]
    chosen = jnp.any(routes[0][:, :, None] == jnp.arange(LANES, dtype=jnp.int32), axis=1).astype(F32)

    q, mixed, mixed_t, lse, n1, small, wqkv, kv_all, wo, w_experts, cots = front(
        blocks, tokens[0], small, query_weight, keyvalue_weight, output_weight, expert_in, expert_out,
        cotangent[0], cosine, sine, start)
    res1, res_grad, attn_grad, d_small, grads, y_parts = expert_layer(
        mixed, tokens[0], small, chosen, wo, w_experts, cots)
    block_out, tokens_grad, d_small, d_keyval, d_experts, d_wo, d_query = backward(
        attn_grad, q, mixed_t, start, lse, tokens[0], cosine, sine, small, d_small,
        kv_all, wo, grads, y_parts, res1, res_grad, n1, wqkv)
    return (block_out[None], tokens_grad[None], d_small[experts], d_query.astype(F32), d_keyval, d_wo.astype(F32),
            d_small[experts + 1], d_small[:experts].T, d_experts[:, :, :width].astype(F32),
            d_experts[:, :, width:].astype(F32))


def solution(mesh):
    token_spec = P("fsdp", ("blk", "head"), None)
    row_spec = P("fsdp", None)
    in_spec = P("blk", "fsdp", None)
    out_spec = P("blk", None, "fsdp")
    return jax.shard_map(
        on_device,
        mesh=mesh,
        in_specs=(token_spec, row_spec, token_spec, token_spec, P("fsdp"), row_spec, row_spec, row_spec, P("fsdp"),
                  row_spec, in_spec, out_spec),
        out_specs=(token_spec, token_spec, P("fsdp"), row_spec, row_spec, row_spec, P("fsdp"), row_spec, in_spec,
                   out_spec),
        check_vma=False,
    )
```

time: 1900 us -> 546 us (0.29)
  waiting for transfers between devices: 758 us -> 0 us
  Pallas kernels: 0 us -> 502 us
  blocking collectives: 499 us -> 0 us
  matrix products: 305 us -> 0 us
  local copies, waits for them, and re-layouts: 171 us -> 8.91 us
  other arithmetic: 87.1 us -> 26 us
  starting transfers between devices: 39.2 us -> 0 us
    pallas_call x0 -> x3, Pallas kernels: none -> 502 us  [the longest x1 251 us: backward(): pl.pallas_call(back_kernel, out_shape=(sds((own_rows, width), BF16), sds(...]
    psum x1 -> x0, blocking collectives: 344 us -> none  [on_device(): lax.psum((shared[0], shared[1], shared[2], shared[3], shared[4], shared[5...]
    reduce_scatter x7 -> x0, waiting for transfers between devices: 332 us -> none  [the longest x1 113 us: on_device(): lax.psum_scatter(grad_expert_in.astype(jnp.bfloat16), 'fsdp', scatter_dim...]
    dot_general x59 -> x0, matrix products: 305 us -> none  [the longest x4 34 us: backward_compute_block(): jnp.einsum('qhd,hkd->hqk', mixed_grad_group, values_here, preferred_eleme...]
    all_to_all x7 -> x0, waiting for transfers between devices: 279 us -> none  [the longest x1 91.6 us: on_device(): lax.all_to_all(input_grad, 'blk', split_axis=0, concat_axis=0, tiled=True)]
    all_gather x6 -> x0, waiting for transfers between devices: 144 us -> none  [the longest x1 51.7 us: on_device(): lax.all_gather(keyval_group, 'blk', axis=0, tiled=True)]
    all_to_all x3 -> x0, blocking collectives: 140 us -> none  [the longest x1 109 us: on_device(): lax.all_to_all(grad_send.reshape(block_count, local_experts, capacity, mo...]
    all_to_all x7 -> x0, starting transfers between devices: 38.3 us -> none  [the longest x1 7.18 us: on_device(): lax.all_to_all(produced, 'blk', split_axis=0, concat_axis=0, tiled=True)]
  transfers between devices with their start and end apart: 21 -> 0, of which waited for: 18 -> 0; matrix products, arithmetic and copies ran while one was open for 13% -> 0% of each run, Pallas kernels for 0% -> 0%
where the time goes in v1:
time: 546 us; the launch traced here: 538 us
  Pallas kernels  502 us (92%)
  other arithmetic  26 us (5%)
  local copies, waits for them, and re-layouts  8.91 us (2%)
    pallas_call x1, Pallas kernels, backward(): pl.pallas_call(back_kernel, out_shape=(sds((own_rows, width), BF16), sds(...  251 us
    pallas_call x1, Pallas kernels, expert_layer(): pl.pallas_call(expert_kernel, out_shape=(sds((own_rows, width), F32), sds...  142 us
    pallas_call x1, Pallas kernels, front(): pl.pallas_call(front_kernel, out_shape=(sds((heads, rows, HEAD), BF16), s...  109 us

profile of v1, /device:TPU:27, one launch (start us, length us, event | category | flops | bytes accessed | tf_op | source)
XLA Modules:
  0.0 538.2 jit_solution(454205636130667522)
XLA Ops:
  0.7 0.1 pad.7.clone
  0.7 1.4 fusion.2
  2.2 3.2 fusion.6.start_ref
  5.4 0.7 broadcast_in_dim.33
  6.1 0.7 broadcast_in_dim.34
  6.8 1.4 maximum_maximum_fusion.small_ref
  8.2 0.9 fusion
  9.1 0.7 convert_element_type.46.chosen_ref
  9.8 1.9 fusion.1
  11.7 1.3 pad_maximum_fusion
  13.0 109.2 %shard_map.195 = (bf16[3,1024,128]{2,1,0:T(8,128)(2,1)}, bf16[1024,384]{1,0:T(8,128)(2,1)}, bf16[384,1024]{1,0:T(8,128)(2,1)}, f32[3,1,1024]{2,1,0:T(1,128)}, bf...) custom-call(bf16[256,1536]{1,0:T(8,128)(2,1)} %bitcast.8, ...), custom_call_target="tpu_custom_call" | custom-call | tf_op jit(solution)/shard_map/pallas_call | solution.py:481
  122.2 142.0 %shard_map.196 = (f32[256,1536]{1,0:T(8,128)}, f32[256,1536]{1,0:T(8,128)}, bf16[256,1536]{1,0:T(8,128)(2,1)}, f32[16,1536]{1,0:T(8,128)}, bf16[2,768,2304]{2,1,...) custom-call(bf16[1024,384]{1,0:T(8,128)(2,1)} %get-tuple-element.34.o_ref, ...), custom_call_target="tpu_custom_call" | custom-call | tf_op jit(solution)/shard_map/pallas_call | solution.py:934
  264.2 251.2 %shard_map.197 = (bf16[256,1536]{1,0:T(8,128)(2,1)}, bf16[256,1536]{1,0:T(8,128)(2,1)}, f32[16,768]{1,0:T(8,128)}, f32[768,512]{1,0:T(8,128)}, bf16[2,768,2304]{...) custom-call(bf16[256,1536]{1,0:T(8,128)(2,1)} %get-tuple-element.39.attn_re, ...), custom_call_target="tpu_custom_call" | custom-call | tf_op jit(solution)/shard_map/pallas_call | solution.py:1504
  515.4 1.5 slice_reduce_fusion
  516.9 1.3 slice_bitcast_fusion
  518.3 4.5 convert_element_type.47
  522.8 0.0 copy-done.1
  522.8 3.0 convert_element_type.48
  525.8 1.7 copy-done
  527.5 2.5 slice_convert_fusion.1
  530.1 5.1 slice_convert_fusion
  535.1 0.9 copy.26
  536.0 0.9 copy.27
  536.9 1.1 copy.28
  (11 shorter events, 0.0 us)
Async XLA Ops:
  515.4 7.4 %copy-start.1 = (bf16[768,1536]{1,0:T(8,128)(2,1)S(1)}, bf16[768,1536]{1,0:T(8,128)(2,1)}, u32[]{:S(2)}) copy-start(bf16[768,1536]{1,0:T(8,128)(2,1)} %get-tuple-element.56) | copy-start | bytes 7077892
  522.8 4.7 copy-start
  530.1 5.1 copy-start.4
  530.1 6.0 %copy-start.3 = (bf16[256,1536]{1,0:T(8,128)(2,1)S(1)}, bf16[256,1536]{1,0:T(8,128)(2,1)}, u32[]{:S(2)}) copy-start(bf16[256,1536]{1,0:T(8,128)(2,1)} %get-tuple-element.52) | copy-start | bytes 2359300
  535.1 1.8 copy-start.2

commit v2 on v1

--- a/solution.py
+++ b/solution.py
@@ -373,17 +373,16 @@
 
         for hh in range(heads):
             q_ref[hh, band, :] = turned(pre[:, hh * HEAD:(hh + 1) * HEAD])
-        kv_ref[me, band, :HEAD] = turned(pre[:, qcols:qcols + HEAD])
-        kv_ref[me, band, HEAD:] = pre[:, qcols + HEAD:].astype(BF16)
+        kv_ref[me, 0, band, :] = turned(pre[:, qcols:qcols + HEAD])
+        kv_ref[me, 1, band, :] = pre[:, qcols + HEAD:].astype(BF16)
         return 0
 
     lax.fori_loop(0, rows // TILE, project, 0)
 
     kvs, kvc = lanes.slots(blocks), lanes.slots(blocks)
-    half_rows = rows // 2
 
     def kv_half(b, core):
-        return kv_ref.at[b, aligned(core * half_rows, half_rows), :]
+        return kv_ref.at[b, core]
 
     lanes.put(kvs + me, kv_half(me, at.c), kv_half(me, at.c), when=me < blocks - 1, blk=me + 1)
     late = [copy_here(wqkv_ref, wqkv_out), copy_here(wo_ref.at[own_half, :], wo_out.at[own_half, :]),
@@ -394,14 +393,14 @@
     acc_ref[...] = jnp.zeros_like(acc_ref)
 
     def transpose_values(b):
-        vt_ref[...] = kv_ref[b, :, HEAD:].astype(F32).T.astype(BF16)
+        vt_ref[...] = kv_ref[b, 1].astype(F32).T.astype(BF16)
 
     transpose_values(me)
     for i in range(rows // TILE):
         n = (i + 1) * TILE
 
         def diagonal(hh, _, i=i, n=n):
-            attend_tile(hh, slice(i * TILE, n), kv_ref[me, :n, :HEAD], vt_ref[:, :n], q_ref, start_ref,
+            attend_tile(hh, slice(i * TILE, n), kv_ref[me, 0, :n, :], vt_ref[:, :n], q_ref, start_ref,
                         m_ref, l_ref, acc_ref, me * rows, me * rows + i * TILE)
             return 0
 
@@ -413,7 +412,7 @@
         def tile(t, _):
             hh, i = t // (rows // TILE), t % (rows // TILE)
             cols = pl.ds(pl.multiple_of(i * TILE, TILE), TILE)
-            attend_tile(hh, cols, kv_ref[b, :, :HEAD], vt_ref[...], q_ref, start_ref,
+            attend_tile(hh, cols, kv_ref[b, 0], vt_ref[...], q_ref, start_ref,
                         m_ref, l_ref, acc_ref, b * rows, None)
             return 0
 
@@ -488,7 +487,7 @@
             sds((rows, width), BF16),
             sds((small.shape[0], width), BF16),
             sds((width, qcols + 2 * HEAD), BF16),
-            sds((blocks, rows, 2 * HEAD), BF16),
+            sds((blocks, 2, rows, HEAD), BF16),
             sds((width, width), BF16),
             sds((2, 2, half, width + half), BF16),
             sds((blocks, own_rows, width), BF16),
@@ -499,7 +498,7 @@
             pltpu.VMEM((rows, width), BF16),
             pltpu.VMEM(small.shape, BF16),
             pltpu.VMEM((width, qcols + 2 * HEAD), BF16),
-            pltpu.VMEM((blocks, rows, 2 * HEAD), BF16),
+            pltpu.VMEM((blocks, 2, rows, HEAD), BF16),
             pltpu.VMEM((heads, 1, rows), F32),
             pltpu.VMEM((heads, 1, rows), F32),
             pltpu.VMEM((heads, HEAD, rows), F32),
@@ -813,36 +812,6 @@
     lax.fori_loop(0, blocks, distance, 0)
     y_copy(me).wait()
 
-    late.settle()
-    total_ref = g_ref if big else w_ref
-
-    def weights_of(e):
-        def rows(i, _):
-            cols = pl.ds(pl.multiple_of(i * tile, tile), tile)
-            for y in range(2):
-                total = mm(xt_ref[y * half:(y + 1) * half, :], dgu_ref[e, :, cols])
-                total_ref[e, y, :, cols] = total.astype(BF16)
-            return 0
-
-        def outs(i, _):
-            for y in range(2):
-                cols = pl.ds(pl.multiple_of(y * half + i * tile, tile), tile)
-                place = pl.ds(pl.multiple_of(width + i * tile, tile), tile)
-                total_ref[e, y, :, place] = mm(gat_ref[e], cot_ref[:, cols]).astype(BF16)
-            return 0
-
-        lax.fori_loop(0, 2 * ffe // tile, rows, 0)
-        lax.fori_loop(0, half // tile, outs, 0)
-
-    chunks = 4
-    piece = half // chunks
-    cores = lanes.slots(chunks)
-    if not big:
-        weights_of(1 - at.c)
-    for k in range(chunks):
-        band = pl.ds(k * piece, piece)
-        lanes.put(cores + k, total_ref.at[1 - at.c, :, band, :], core_land.at[:, band, :], head=at.sib)
-
     def add(b, rows):
         if big:
             move(dx_ref.at[b, rows, :], dx_stage.at[rows, :])
@@ -852,6 +821,37 @@
         else:
             dx_ref[b, rows, :] = (dx_ref[b, rows, :].astype(F32) + land_ref[b, rows, :].astype(F32)).astype(BF16)
 
+    late.settle()
+    total_ref = g_ref if big else w_ref
+
+    def weights_of(e):
+        def rows(i, _):
+            cols = pl.ds(pl.multiple_of(i * tile, tile), tile)
+            for y in range(2):
+                total = mm(xt_ref[y * half:(y + 1) * half, :], dgu_ref[e, :, cols])
+                total_ref[e, y, :, cols] = total.astype(BF16)
+            return 0
+
+        def outs(i, _):
+            for y in range(2):
+                cols = pl.ds(pl.multiple_of(y * half + i * tile, tile), tile)
+                place = pl.ds(pl.multiple_of(width + i * tile, tile), tile)
+                total_ref[e, y, :, place] = mm(gat_ref[e], cot_ref[:, cols]).astype(BF16)
+            return 0
+
+        lax.fori_loop(0, 2 * ffe // tile, rows, 0)
+        lax.fori_loop(0, half // tile, outs, 0)
+
+    chunks = 4
+    piece = half // chunks
+    cores = lanes.slots(chunks)
+    back.relay(0, 1, add)
+    if not big:
+        weights_of(1 - at.c)
+    for k in range(chunks):
+        band = pl.ds(k * piece, piece)
+        lanes.put(cores + k, total_ref.at[1 - at.c, :, band, :], core_land.at[:, band, :], head=at.sib)
+
     def core_sum(k):
         band = pl.ds(k * piece, piece)
         lanes.arrived(cores + k, core_land.at[:, band, :], head=at.sib)
@@ -860,11 +860,12 @@
             total = total_ref[at.c, y, band, :].astype(F32) + stage_ref[y].astype(F32)
             total_ref[at.c, y, band, :] = total.astype(BF16)
 
-    for phase in range(2):
-        for d in range(1, blocks):
-            back.relay(phase, d, add)
+    for d in range(2, blocks):
+        back.relay(0, d, add)
     if not big:
         weights_of(at.c)
+    for d in range(1, blocks):
+        back.relay(1, d, add)
     for k in range(chunks):
         core_sum(k)
     keep = pltpu.make_async_copy(total_ref.at[at.c], sums_out, load_sem.at[0])
@@ -1118,11 +1119,10 @@
         yp_ref, dkv_land, dkv_sib, dwo_z, kv_ref, *rest = rest
     (dq_ref, dk_ref, dv_ref, kt_ref, delta_ref, do_ref, ag_ref, wo_ref, dwo_ref, dwo_y, dwo_land,
      own_ref, ey_ref, ex_ref, acc_ref, y_other, w_ref, dpre_ref, dn_sib, dn_x, dw_ref, dw_y, dw_z,
-     sm_ref, sm_a, sm_b, sm_y, sm_z, land_ref, dkv_ref, load_sem, keep_sem, send_sem, recv_sem) = rest
+     sm_ref, sm_a, sm_b, sm_y, sm_z, land_ref, dkv_ref, n1t_ref, load_sem, keep_sem, send_sem, recv_sem) = rest
     heads, rows, _ = q_ref.shape
     own_rows, width = attn_ref.shape
     half = width // 2
-    half_rows = rows // 2
     qcols = heads * HEAD
     gain_row = 2 * blocks
     at = Place(blocks)
@@ -1133,7 +1133,7 @@
     output = OutputSums(at, lanes, dwo_ref, dwo_y, dwo_z, dwo_land)
     sums = ColumnSum(at, lanes, yp_ref, y_land)
     experts.load()
-    forward, near, far, passed = gather_heads(at, lanes, attn_ref, ag_ref)
+    forward, near, far, _ = gather_heads(at, lanes, attn_ref, ag_ref)
 
     def load(src, dst, sem):
         copy = pltpu.make_async_copy(src, dst, load_sem.at[sem])
@@ -1177,10 +1177,19 @@
         for hh in range(heads):
             do_ref[hh, band, :] = grad[:, hh * HEAD:(hh + 1) * HEAD]
 
+    def turn(i):
+        band = slice(i * own_rows, (i + 1) * own_rows)
+        move(n1_hbm.at[band, :], y_other)
+        n1t_ref[:, band] = y_other[...].astype(F32).T.astype(BF16)
+
     ag_ref[aligned(at.h * own_rows, own_rows), :] = attn_ref[...]
     mix_back(at.h)
+    turn(0)
     near()
     mix_back(at.sib)
+    for i in range(1, rows // own_rows):
+        turn(i)
+    experts.to_x(0)
     forward()
     mix_back(at.xn)
     far()
@@ -1194,9 +1203,8 @@
 
     lax.fori_loop(0, width // step, weight_back, 0)
     output.to_z()
-    lanes.settle(passed[0])
-    n1_load = load(n1_hbm, ag_ref, 2)
-    w_load = load(w_hbm, w_ref, 3)
+    kv_from = pl.ds(pl.multiple_of(qcols + at.c * HEAD, HEAD), HEAD)
+    w_loads = [load(w_hbm.at[:, :qcols], w_ref.at[:, :qcols], 2), load(w_hbm.at[:, kv_from], w_ref.at[:, qcols:], 3)]
     dq_ref[...] = jnp.zeros_like(dq_ref)
     for hh in range(heads):
         prod = do_ref[hh].astype(F32).T * ot_ref[hh * HEAD:(hh + 1) * HEAD, :].astype(F32)
@@ -1204,11 +1212,10 @@
     if not big:
         kv_load.wait()
 
-    for k in (0, 1):
-        experts.to_x(k)
+    experts.to_x(1)
     beside = [[(experts.to_x, 2), (experts.share, 0)],
-              [(experts.to_x, 3), (experts.share, 1), (experts.to_x, 4)],
-              [(experts.to_x, 5), (experts.share, 2), (experts.share, 3)]]
+              [(experts.to_x, 3), (experts.share, 1)],
+              [(experts.to_x, 4), (experts.share, 2)]]
 
     def advance():
         for f, k in (beside.pop(0) if beside else ()):
@@ -1218,14 +1225,14 @@
         if big:
             move(kv_in.at[b], kv_stage)
         kv = kv_stage if big else kv_ref.at[b]
-        kt_ref[...] = kv[:, :HEAD].astype(F32).T.astype(BF16)
+        kt_ref[...] = kv[0].astype(F32).T.astype(BF16)
         dk_ref[...] = jnp.zeros_like(dk_ref)
         dv_ref[...] = jnp.zeros_like(dv_ref)
         return kv
 
     def closing(b, kv):
-        kv[:, :HEAD] = (dk_ref[...] * SCORE_SCALE).astype(BF16)
-        kv[:, HEAD:] = dv_ref[...].astype(BF16)
+        kv[0] = (dk_ref[...] * SCORE_SCALE).astype(BF16)
+        kv[1] = dv_ref[...].astype(BF16)
         if big:
             move(kv_stage, kv_ref.at[b])
 
@@ -1235,21 +1242,17 @@
         def tile(t, _):
             hh, i = t // (rows // TILE), t % (rows // TILE)
             cols = pl.ds(pl.multiple_of(i * TILE, TILE), TILE)
-            unattend_tile(hh, cols, kv[:, :HEAD], kv[:, HEAD:], kt_ref[...], q_ref, do_ref,
+            unattend_tile(hh, cols, kv[0], kv[1], kt_ref[...], q_ref, do_ref,
                           start_ref, lse_ref, delta_ref, dq_ref, dk_ref, dv_ref, b * rows, None)
             return 0
 
         lax.fori_loop(0, heads * (rows // TILE), tile, 0)
         closing(b, kv)
 
-    def half_of(core):
-        return aligned(core * half_rows, half_rows)
-
-    mine, other = half_of(at.c), half_of(1 - at.c)
     pair, column = lanes.slots(blocks), lanes.slots(blocks)
 
     def to_sibling(b, when):
-        lanes.put(pair + b, kv_ref.at[b, other, :], dkv_sib.at[b], when=when, head=at.sib)
+        lanes.put(pair + b, kv_ref.at[b, 1 - at.c], dkv_sib.at[b], when=when, head=at.sib)
 
     def to_column(b):
         lanes.arrived(pair + b, dkv_sib.at[b], when=b < me, head=at.sib)
@@ -1258,13 +1261,13 @@
         def _():
             came = fetch(dkv_stage)(dkv_sib.at[b])
             if big:
-                move(kv_ref.at[b, mine, :], kv_stage.at[mine, :])
+                move(kv_ref.at[b, at.c], kv_stage.at[at.c])
             kv = kv_stage if big else kv_ref.at[b]
-            kv[mine, :] = (kv[mine, :].astype(F32) + came[...].astype(F32)).astype(BF16)
+            kv[at.c] = (kv[at.c].astype(F32) + came[...].astype(F32)).astype(BF16)
             if big:
-                move(kv_stage.at[mine, :], kv_ref.at[b, mine, :])
-
-        lanes.put(column + me, kv_ref.at[b, mine, :], dkv_land.at[me], when=b < me, blk=b)
+                move(kv_stage.at[at.c], kv_ref.at[b, at.c])
+
+        lanes.put(column + me, kv_ref.at[b, at.c], dkv_land.at[me], when=b < me, blk=b)
 
     for b in range(blocks - 1):
         pl.when(b < me)(functools.partial(block, b))
@@ -1282,7 +1285,7 @@
         n = (i + 1) * TILE
 
         def diagonal(hh, _, i=i, n=n):
-            unattend_tile(hh, slice(i * TILE, n), kv_own[:n, :HEAD], kv_own[:n, HEAD:], kt_ref[:, :n], q_ref, do_ref,
+            unattend_tile(hh, slice(i * TILE, n), kv_own[0, :n, :], kv_own[1, :n, :], kt_ref[:, :n], q_ref, do_ref,
                           start_ref, lse_ref, delta_ref, dq_ref, dk_ref, dv_ref,
                           me * rows, me * rows + i * TILE)
             return 0
@@ -1290,27 +1293,26 @@
         lax.fori_loop(0, heads, diagonal, 0)
     closing(me, kv_own)
     to_sibling(me, None)
+    experts.to_x(5)
     for d in range(1, blocks):
         sums.relay(1, d, add)
 
-    def unrotate(u, band):
-        return u * cos_ref[band, :] - pltpu.roll(u, HEAD // 2, 1) * sin_ref[band, :]
+    def unrotate(u):
+        return u * cos_ref[...] - pltpu.roll(u, HEAD // 2, 1) * sin_ref[...]
 
     for hh in range(heads):
-        dpre_ref[:, hh * HEAD:(hh + 1) * HEAD] = unrotate((dq_ref[hh] * SCORE_SCALE).T, slice(None)).astype(BF16)
-    n1_load.wait()
-    w_load.wait()
-    n1_ref = ag_ref
+        dpre_ref[:, hh * HEAD:(hh + 1) * HEAD] = unrotate((dq_ref[hh] * SCORE_SCALE).T).astype(BF16)
+    for w_load in w_loads:
+        w_load.wait()
     parts = 4
     part = half // parts
     band_rows = 256
-    query_cols, keyval_cols = slice(0, qcols), slice(qcols, qcols + 2 * HEAD)
+    query_cols, keyval_cols = slice(0, qcols), slice(qcols, qcols + HEAD)
 
     def weight_half(y, cols_out):
         def body(i, _):
-            cols = pl.ds(pl.multiple_of(y * half + i * band_rows, band_rows), band_rows)
-            dw_ref[aligned(y * half + i * band_rows, band_rows), cols_out] = (
-                mm(n1_ref[:, cols], dpre_ref[:, cols_out], TN).astype(BF16))
+            band = aligned(y * half + i * band_rows, band_rows)
+            dw_ref[band, cols_out] = mm(n1t_ref[band, :], dpre_ref[:, cols_out]).astype(BF16)
             return 0
 
         lax.fori_loop(0, half // band_rows, body, 0)
@@ -1329,9 +1331,14 @@
     weight_to_y(0, query_cols)
     experts.to_x(6)
 
-    dpre_ref[other, qcols:] = jnp.zeros((half_rows, 2 * HEAD), BF16)
-    dkv_ref[:, :HEAD] = dk_ref[mine, :] * SCORE_SCALE
-    dkv_ref[:, HEAD:] = dv_ref[mine, :]
+    @pl.when(at.c == 0)
+    def _():
+        dkv_ref[...] = dk_ref[...] * SCORE_SCALE
+
+    @pl.when(at.c == 1)
+    def _():
+        dkv_ref[...] = dv_ref[...]
+
     lanes.arrived(pair + me, dkv_sib.at[me], head=at.sib)
     dkv_ref[...] += fetch(dkv_stage)(dkv_sib.at[me])[...].astype(F32)
     for z in range(1, blocks):
@@ -1340,8 +1347,7 @@
             lanes.arrived(column + z, dkv_land.at[z], blk=z)
             dkv_ref[...] += fetch(dkv_stage)(dkv_land.at[z])[...].astype(F32)
 
-    dpre_ref[mine, qcols:qcols + HEAD] = unrotate(dkv_ref[:, :HEAD], mine).astype(BF16)
-    dpre_ref[mine, qcols + HEAD:] = dkv_ref[:, HEAD:].astype(BF16)
+    dpre_ref[:, qcols:] = jnp.where(at.c == 0, unrotate(dkv_ref[...]), dkv_ref[...]).astype(BF16)
     weight_to_y(1, keyval_cols)
 
     def input_part(head):
@@ -1361,6 +1367,7 @@
     dn_ref(1)[...] = (input_part(at.xn) + dn_sib[0].astype(F32)).astype(BF16)
     lanes.put(across, dn_ref(1), dn_x, head=at.xn)
     experts.to_x(7)
+    experts.share(3)
     experts.share(4)
     weight_half(at.y, slice(None))
     output.to_y(fetch(dwo_stage))
@@ -1468,10 +1475,8 @@
         lanes.arrived(cf + q, place(at.xs, q), head=at.sib)
     for head in range(4):
         keeps.append(load(land_ref.at[head, :, :qcols], query_out.at[:, head * qcols:(head + 1) * qcols], 1 + head))
-    for g in range(KEYVALUE_HEADS):
-        both = land_ref[2 * g, :, qcols:].astype(F32) + land_ref[2 * g + 1, :, qcols:].astype(F32)
-        kv_out[:, g * HEAD:(g + 1) * HEAD] = both[:, :HEAD]
-        kv_out[:, (KEYVALUE_HEADS + g) * HEAD:(KEYVALUE_HEADS + g + 1) * HEAD] = both[:, HEAD:]
+        column_of = (head % 2 * KEYVALUE_HEADS + head // 2) * HEAD
+        keeps.append(load(land_ref.at[head, :, qcols:], kv_out.at[:, column_of:column_of + HEAD], 6 + head))
     experts.finish()
     for keep in keeps:
         keep.wait()
@@ -1485,19 +1490,19 @@
     own_rows, width = attn_grad.shape
     qcols = heads * HEAD
     _, half, wide = grads.shape
-    cols = w.shape[1]
+    cols = qcols + HEAD
     srows = small.shape[0]
     n = ExpertSums.CHUNKS
     vm = pl.BlockSpec(memory_space=pltpu.VMEM)
     hbm = pl.BlockSpec(memory_space=pl.ANY)
     part = qcols // OutputSums.PARTS
     sds = jax.ShapeDtypeStruct
-    column = [((blocks, own_rows, width), BF16), ((blocks, rows // 2, 2 * HEAD), BF16),
-              ((blocks, rows // 2, 2 * HEAD), BF16), ((blocks, part, width), BF16), (kv.shape, BF16)]
+    column = [((blocks, own_rows, width), BF16), ((blocks, rows, HEAD), BF16),
+              ((blocks, rows, HEAD), BF16), ((blocks, part, width), BF16), (kv.shape, BF16)]
     if blocks > 4:
         extra_out, extra_spec = tuple(sds(*c) for c in column), [hbm] * 5
-        extra_scratch = [pltpu.VMEM((rows // 2, 2 * HEAD), BF16), pltpu.VMEM((part, width), BF16),
-                         pltpu.VMEM((own_rows, width), BF16), pltpu.VMEM((rows, 2 * HEAD), BF16)]
+        extra_scratch = [pltpu.VMEM((rows, HEAD), BF16), pltpu.VMEM((part, width), BF16),
+                         pltpu.VMEM((own_rows, width), BF16), pltpu.VMEM((2, rows, HEAD), BF16)]
     else:
         extra_out, extra_spec = (), []
         extra_scratch = [pltpu.VMEM(*c) for c in column]
@@ -1507,14 +1512,14 @@
             sds((own_rows, width), BF16),
             sds((own_rows, width), BF16),
             sds((srows, half), F32),
-            sds((half, 2 * KEYVALUE_HEADS * HEAD), F32),
+            sds((half, 2 * KEYVALUE_HEADS * HEAD), BF16),
             sds((2, half, wide), BF16),
             sds((2 * qcols, width), BF16),
             sds((half, rows // own_rows * qcols), BF16),
             sds((blocks + 1, own_rows, width), BF16),
         ) + extra_out,
         in_specs=[vm] * 10 + [hbm] * 8,
-        out_specs=[vm] * 4 + [hbm] * 4 + extra_spec,
+        out_specs=[vm] * 3 + [hbm] * 5 + extra_spec,
         scratch_shapes=extra_scratch + [
             pltpu.VMEM((heads, HEAD, rows), F32),
             pltpu.VMEM((rows, HEAD), F32),
@@ -1545,8 +1550,9 @@
             pltpu.VMEM((srows, half), F32),
             pltpu.VMEM((blocks, srows, half), F32),
             pltpu.VMEM((rows // own_rows, half, cols), BF16),
-            pltpu.VMEM((rows // 2, 2 * HEAD), F32),
-            pltpu.SemaphoreType.DMA((6,)),
+            pltpu.VMEM((rows, HEAD), F32),
+            pltpu.VMEM((width, rows), BF16),
+            pltpu.SemaphoreType.DMA((10,)),
             pltpu.SemaphoreType.DMA((n,)),
         ] + semaphores(blocks),
         compiler_params=pltpu.CompilerParams(
@@ -1585,7 +1591,7 @@
     block_out, tokens_grad, d_small, d_keyval, d_experts, d_wo, d_query = backward(
         attn_grad, q, mixed_t, start, lse, tokens[0], cosine, sine, small, d_small,
         kv_all, wo, grads, y_parts, res1, res_grad, n1, wqkv)
-    return (block_out[None], tokens_grad[None], d_small[experts], d_query.astype(F32), d_keyval, d_wo.astype(F32),
+    return (block_out[None], tokens_grad[None], d_small[experts], d_query.astype(F32), d_keyval.astype(F32), d_wo.astype(F32),
             d_small[experts + 1], d_small[:experts].T, d_experts[:, :, :width].astype(F32),
             d_experts[:, :, width:].astype(F32))
 

time: 546 us -> 533 us (0.976)
  Pallas kernels: 502 us -> 490 us
    pallas_call x1, Pallas kernels: 251 us -> 230 us  [backward(): pl.pallas_call(back_kernel, out_shape=(sds((own_rows, width), BF16), sds(...]
    pallas_call x1, Pallas kernels: 142 us -> 151 us  [expert_layer(): pl.pallas_call(expert_kernel, out_shape=(sds((own_rows, width), F32), sds...]
where the time goes in v2:
time: 533 us; the launch traced here: 525 us
  Pallas kernels  490 us (92%)
  other arithmetic  28.6 us (5%)
  local copies, waits for them, and re-layouts  6 us (1%)
    pallas_call x1, Pallas kernels, backward(): pl.pallas_call(back_kernel, out_shape=(sds((own_rows, width), BF16), sds(...  230 us
    pallas_call x1, Pallas kernels, expert_layer(): pl.pallas_call(expert_kernel, out_shape=(sds((own_rows, width), F32), sds...  151 us
    pallas_call x1, Pallas kernels, front(): pl.pallas_call(front_kernel, out_shape=(sds((heads, rows, HEAD), BF16), s...  109 us

profile of v2, /device:TPU:27, one launch (start us, length us, event | category | flops | bytes accessed | tf_op | source)
XLA Modules:
  0.0 525.2 jit_solution(12812190577041242938)
XLA Ops:
  0.7 0.1 pad.7.clone
  0.7 1.4 fusion.2
  2.2 3.2 fusion.6.start_ref
  5.4 0.7 broadcast_in_dim.33
  6.1 0.7 broadcast_in_dim.34
  6.8 1.4 maximum_maximum_fusion.small_ref
  8.2 0.9 fusion
  9.1 0.7 convert_element_type.49.chosen_ref
  9.8 1.9 fusion.1
  11.7 1.3 pad_maximum_fusion
  13.0 109.1 %shard_map.195 = (bf16[3,1024,128]{2,1,0:T(8,128)(2,1)}, bf16[1024,384]{1,0:T(8,128)(2,1)}, bf16[384,1024]{1,0:T(8,128)(2,1)}, f32[3,1,1024]{2,1,0:T(1,128)}, bf...) custom-call(bf16[256,1536]{1,0:T(8,128)(2,1)} %bitcast.8, ...), custom_call_target="tpu_custom_call" | custom-call | tf_op jit(solution)/shard_map/pallas_call | solution.py:480
  122.1 150.8 %shard_map.196 = (f32[256,1536]{1,0:T(8,128)}, f32[256,1536]{1,0:T(8,128)}, bf16[256,1536]{1,0:T(8,128)(2,1)}, f32[16,1536]{1,0:T(8,128)}, bf16[2,768,2304]{2,1,...) custom-call(bf16[1024,384]{1,0:T(8,128)(2,1)} %get-tuple-element.34.o_ref, ...), custom_call_target="tpu_custom_call" | custom-call | tf_op jit(solution)/shard_map/pallas_call | solution.py:935
  273.0 229.7 %shard_map.197 = (bf16[256,1536]{1,0:T(8,128)(2,1)}, bf16[256,1536]{1,0:T(8,128)(2,1)}, f32[16,768]{1,0:T(8,128)}, bf16[768,512]{1,0:T(8,128)(2,1)}, bf16[2,768,...) custom-call(bf16[256,1536]{1,0:T(8,128)(2,1)} %get-tuple-element.39.a, ...), custom_call_target="tpu_custom_call" | custom-call | tf_op jit(solution)/shard_map/pallas_call | solution.py:1509
  502.7 1.4 slice_reduce_fusion
  504.1 1.3 slice_bitcast_fusion
  505.5 2.6 convert_element_type.51
  508.1 4.6 convert_element_type.50
  512.8 2.8 convert_element_type.52
  515.6 0.0 slice-done
  515.6 2.5 slice_convert_fusion.1
  518.1 5.1 slice_convert_fusion
  523.2 0.9 copy.25
  524.1 0.0 copy-done.1
  524.1 0.9 copy.26
  (12 shorter events, 0.0 us)
Async XLA Ops:
  505.5 7.3 %copy-start = (bf16[768,1536]{1,0:T(8,128)(2,1)S(1)}, bf16[768,1536]{1,0:T(8,128)(2,1)}, u32[]{:S(2)}) copy-start(bf16[768,1536]{1,0:T(8,128)(2,1)} %get-tuple-element.56) | copy-start | bytes 7077892
  505.5 10.1 %slice-start = ((s8[7077888]{0:T(1024)(128)(4,1)}), s8[4194304]{0:T(1024)(128)(4,1)S(1)}, s32[]{:S(2)}) async-start(s8[7077888]{0:T(1024)(128)(4,1)} %bitcast.11), calls=%async_computation | async-start | bytes 8388608
  508.1 7.5 %slice-start.1 = ((s8[7077888]{0:T(1024)(128)(4,1)}), s8[2883584]{0:T(1024)(128)(4,1)S(1)}, s32[]{:S(2)}) async-start(s8[7077888]{0:T(1024)(128)(4,1)} %bitcast.11), calls=%async_computation.1 | async-start | bytes 5767168
  518.1 5.1 copy-start.2
  518.1 5.9 %copy-start.1 = (bf16[256,1536]{1,0:T(8,128)(2,1)S(1)}, bf16[256,1536]{1,0:T(8,128)(2,1)}, u32[]{:S(2)}) copy-start(bf16[256,1536]{1,0:T(8,128)(2,1)} %get-tuple-element.52) | copy-start | bytes 2359300

commit v3 on v2

--- a/solution.py
+++ b/solution.py
@@ -17,6 +17,7 @@
 LOG2E = 1.4426950408889634
 SCORE_LOG2 = HEAD ** (-0.5) * LOG2E
 SCORE_SCALE = HEAD ** (-0.5)
+LN2 = 1.0 / LOG2E
 TILE = 256
 BF16 = jnp.bfloat16
 F32 = jnp.float32
@@ -41,12 +42,11 @@
 
 
 def score_tile(key_rows, q_tile, start_row, first_key, q_first):
-    scores = mm(key_rows, q_tile, NT) * SCORE_LOG2
-    key_pos = first_key + lax.broadcasted_iota(jnp.int32, scores.shape, 0)
-    allowed = key_pos >= start_row
+    scores = mm(key_rows, q_tile, NT)
+    key_row = lax.broadcasted_iota(jnp.int32, scores.shape, 0)
+    allowed = key_row >= start_row - first_key
     if q_first is not None:
-        q_pos = q_first + lax.broadcasted_iota(jnp.int32, scores.shape, 1)
-        allowed = allowed & (key_pos <= q_pos)
+        allowed = allowed & (key_row - lax.broadcasted_iota(jnp.int32, scores.shape, 1) <= q_first - first_key)
     return jnp.where(allowed, scores, MASKED)
 
 
@@ -288,20 +288,24 @@
     forward, near, far, _ = gather_heads(at, lanes, x_ref, xg_ref)
     g = at.x
     q_from = pl.ds(pl.multiple_of(at.h * qcols, HEAD), qcols)
-    k_from = pl.ds(pl.multiple_of(g * HEAD, HEAD), HEAD)
-    v_from = pl.ds(pl.multiple_of((KEYVALUE_HEADS + g) * HEAD, HEAD), HEAD)
-    columns = ((wq_hbm.at[:, q_from], slice(0, qcols)), (wkv_hbm.at[:, k_from], slice(qcols, qcols + HEAD)),
-               (wkv_hbm.at[:, v_from], slice(qcols + HEAD, qcols + 2 * HEAD)))
+    kv_from = pl.ds(pl.multiple_of((at.c * KEYVALUE_HEADS + g) * HEAD, HEAD), HEAD)
+
+    def kv_cols(core):
+        return pl.ds(pl.multiple_of(qcols + core * HEAD, HEAD), HEAD)
+
+    columns = ((wq_hbm.at[:, q_from], slice(0, qcols)), (wkv_hbm.at[:, kv_from], kv_cols(at.c)))
 
     def weight_rows(y, cols):
         return wqkv_ref.at[aligned(y * half, half), cols]
 
-    ws = lanes.slots(3)
-    for i, (src, cols) in enumerate(columns):
+    ws, wc = lanes.slots(2), lanes.slots()
+    for i, (src, cols) in reversed(list(enumerate(columns))):
         lanes.put(ws + i, src, weight_rows(at.y, cols), fsdp=at.oy)
     smalls = lanes.slots()
     lanes.put(smalls, small_ref, small_land, fsdp=at.oy)
-    own_weights = [copy_here(src, weight_rows(at.y, cols)) for src, cols in columns]
+    kv_other = pl.ds(pl.multiple_of(((1 - at.c) * KEYVALUE_HEADS + g) * HEAD, HEAD), HEAD)
+    own_weights = [copy_here(src, weight_rows(at.y, cols))
+                   for src, cols in columns + ((wkv_hbm.at[:, kv_other], kv_cols(1 - at.c)),)]
     cots = Column(at, lanes, cot_ref)
     own_half = pl.ds(pl.multiple_of(at.y * half, half), half)
     cot_load = copy_here(cot_hbm, cot_ref.at[me])
@@ -353,8 +357,11 @@
     norm(at.xs, gathered(at.xs))
     for copy in own_weights:
         copy.wait()
-    for i, (_, cols) in enumerate(columns):
+    for i, (_, cols) in reversed(list(enumerate(columns))):
         lanes.arrived(ws + i, weight_rows(at.oy, cols), fsdp=at.oy)
+        if i == 1:
+            lanes.put(wc, weight_rows(at.oy, cols), weight_rows(at.oy, cols), head=at.sib)
+    lanes.arrived(wc, weight_rows(at.oy, kv_cols(1 - at.c)), head=at.sib)
     wo_load.wait()
     shared_wo.begin(0)
     for load in w_loads:
@@ -372,7 +379,7 @@
             return (u * cosine + pltpu.roll(u, HEAD // 2, 1) * sine).astype(BF16)
 
         for hh in range(heads):
-            q_ref[hh, band, :] = turned(pre[:, hh * HEAD:(hh + 1) * HEAD])
+            q_ref[hh, band, :] = turned(pre[:, hh * HEAD:(hh + 1) * HEAD] * SCORE_LOG2)
         kv_ref[me, 0, band, :] = turned(pre[:, qcols:qcols + HEAD])
         kv_ref[me, 1, band, :] = pre[:, qcols + HEAD:].astype(BF16)
         return 0
@@ -1039,7 +1046,7 @@
         self.rows = grad.shape[0] // self.PARTS
         self.ys = lanes.slots()
         self.zr, self.zg = lanes.slots(at.blocks), lanes.slots(self.PARTS)
-        self.xg, self.cg = lanes.slots(self.PARTS), lanes.slots(self.PARTS)
+        self.xg, self.cg = lanes.slots(), lanes.slots(self.PARTS)
         self.owner, self.giver = at.y == at.x, at.y != at.x
         self.summer = at.z < self.PARTS
         self.part = at.z % self.PARTS
@@ -1080,26 +1087,26 @@
             self.out[at_rows, :] = total.astype(BF16)
 
         place = self.place(at.c, p)
+        self.lanes.put(self.xg, place, place, when=ready, head=at.xn)
+        self.spread(ready)
+
+    def spread(self, ready):
+        at, place = self.at, self.place(self.at.c, self.part)
         for z in at.others():
-            self.lanes.put(self.zg + p, place, place, when=ready, blk=z)
-        self.lanes.put(self.xg + p, place, place, when=ready, head=at.xn)
-        self.lanes.put(self.cg + p, place, place, when=ready, head=at.sib)
+            self.lanes.put(self.zg + self.part, place, place, when=ready, blk=z)
+        self.lanes.put(self.cg + self.part, place, place, when=ready, head=at.sib)
+
+    def take_over(self):
+        ready = self.summer & self.giver
+        self.lanes.arrived(self.xg, self.place(self.at.c, self.part), when=ready, head=self.at.xn)
+        self.spread(ready)
 
     def pass_on(self):
         at = self.at
         for p in range(self.PARTS):
-            place = self.place(at.c, p)
-            later = self.owner & (at.z != p)
+            place, later = self.place(at.c, p), at.z != p
             self.lanes.arrived(self.zg + p, place, when=later, blk=p)
-            self.lanes.put(self.xg + p, place, place, when=later, head=at.xn)
             self.lanes.put(self.cg + p, place, place, when=later, head=at.sib)
-
-    def take_over(self):
-        at = self.at
-        for p in range(self.PARTS):
-            place = self.place(at.c, p)
-            self.lanes.arrived(self.xg + p, place, when=self.giver, head=at.xn)
-            self.lanes.put(self.cg + p, place, place, when=self.giver, head=at.sib)
 
     def finish(self):
         at = self.at
@@ -1231,7 +1238,7 @@
         return kv
 
     def closing(b, kv):
-        kv[0] = (dk_ref[...] * SCORE_SCALE).astype(BF16)
+        kv[0] = (dk_ref[...] * LN2).astype(BF16)
         kv[1] = dv_ref[...].astype(BF16)
         if big:
             move(kv_stage, kv_ref.at[b])
@@ -1333,7 +1340,7 @@
 
     @pl.when(at.c == 0)
     def _():
-        dkv_ref[...] = dk_ref[...] * SCORE_SCALE
+        dkv_ref[...] = dk_ref[...] * LN2
 
     @pl.when(at.c == 1)
     def _():
@@ -1441,7 +1448,7 @@
     lanes.arrived(sa, sm_a, head=at.sib)
     sm_a[...] = sm_a[...] + sm_ref[...]
     lanes.put(sb, sm_a, sm_b, head=at.xn)
-    output.pass_on()
+    output.take_over()
     experts.share(7)
 
     lanes.arrived(sb, sm_b, head=at.xn)
@@ -1458,7 +1465,7 @@
     sm_z[at.z] = sm_b[:, mine_cols] + sm_y[...]
     for z in at.others():
         lanes.put(sz + at.z, sm_z.at[at.z], sm_z.at[at.z], blk=z)
-    output.take_over()
+    output.pass_on()
     for q in range(parts):
         lanes.arrived(xg + q, place(at.xn, q), head=at.xn)
         lanes.put(cf + q, place(at.xn, q), place(at.xn, q), head=at.sib)

time: 533 us -> 524 us (0.983)
  Pallas kernels: 490 us -> 481 us
    pallas_call x1, Pallas kernels: 230 us -> 221 us  [backward(): pl.pallas_call(back_kernel, out_shape=(sds((own_rows, width), BF16), sds(...]
where the time goes in v3:
time: 524 us; the launch traced here: 517 us
  Pallas kernels  481 us (92%)
  other arithmetic  28.6 us (5%)
  local copies, waits for them, and re-layouts  6 us (1%)
    pallas_call x1, Pallas kernels, backward(): pl.pallas_call(back_kernel, out_shape=(sds((own_rows, width), BF16), sds(...  221 us
    pallas_call x1, Pallas kernels, expert_layer(): pl.pallas_call(expert_kernel, out_shape=(sds((own_rows, width), F32), sds...  152 us
    pallas_call x1, Pallas kernels, front(): pl.pallas_call(front_kernel, out_shape=(sds((heads, rows, HEAD), BF16), s...  108 us

profile of v3, /device:TPU:27, one launch (start us, length us, event | category | flops | bytes accessed | tf_op | source)
XLA Modules:
  0.0 516.6 jit_solution(9911400114783636513)
XLA Ops:
  0.7 0.1 pad.7.clone
  0.7 1.4 fusion.2
  2.2 3.2 fusion.6.start_ref
  5.4 0.7 broadcast_in_dim.33
  6.1 0.7 broadcast_in_dim.34
  6.8 1.4 maximum_maximum_fusion.small_ref
  8.2 0.9 fusion
  9.1 0.7 convert_element_type.49.chosen_ref
  9.8 1.9 fusion.1
  11.7 1.3 pad_maximum_fusion
  13.0 108.0 %shard_map.195 = (bf16[3,1024,128]{2,1,0:T(8,128)(2,1)}, bf16[1024,384]{1,0:T(8,128)(2,1)}, bf16[384,1024]{1,0:T(8,128)(2,1)}, f32[3,1,1024]{2,1,0:T(1,128)}, bf...) custom-call(bf16[256,1536]{1,0:T(8,128)(2,1)} %bitcast.8, ...), custom_call_target="tpu_custom_call" | custom-call | tf_op jit(solution)/shard_map/pallas_call | solution.py:487
  121.0 151.6 %shard_map.196 = (f32[256,1536]{1,0:T(8,128)}, f32[256,1536]{1,0:T(8,128)}, bf16[256,1536]{1,0:T(8,128)(2,1)}, f32[16,1536]{1,0:T(8,128)}, bf16[2,768,2304]{2,1,...) custom-call(bf16[1024,384]{1,0:T(8,128)(2,1)} %get-tuple-element.34.o_ref, ...), custom_call_target="tpu_custom_call" | custom-call | tf_op jit(solution)/shard_map/pallas_call | solution.py:942
  272.6 221.5 %shard_map.197 = (bf16[256,1536]{1,0:T(8,128)(2,1)}, bf16[256,1536]{1,0:T(8,128)(2,1)}, f32[16,768]{1,0:T(8,128)}, bf16[768,512]{1,0:T(8,128)(2,1)}, bf16[2,768,...) custom-call(bf16[256,1536]{1,0:T(8,128)(2,1)} %get-tuple-element.39.a, ...), custom_call_target="tpu_custom_call" | custom-call | tf_op jit(solution)/shard_map/pallas_call | solution.py:1516
  494.1 1.4 slice_reduce_fusion
  495.5 1.3 slice_bitcast_fusion
  496.9 2.6 convert_element_type.51
  499.5 4.6 convert_element_type.50
  504.2 0.0 copy-done
  504.2 2.8 convert_element_type.52
  507.0 2.5 slice_convert_fusion.1
  509.5 5.1 slice_convert_fusion
  514.6 0.9 copy.25
  515.5 0.0 copy-done.1
  515.5 0.9 copy.26
  (12 shorter events, 0.0 us)
Async XLA Ops:
  496.9 7.3 %copy-start = (bf16[768,1536]{1,0:T(8,128)(2,1)S(1)}, bf16[768,1536]{1,0:T(8,128)(2,1)}, u32[]{:S(2)}) copy-start(bf16[768,1536]{1,0:T(8,128)(2,1)} %get-tuple-element.56) | copy-start | bytes 7077892
  496.9 10.1 %slice-start = ((s8[7077888]{0:T(1024)(128)(4,1)}), s8[4194304]{0:T(1024)(128)(4,1)S(1)}, s32[]{:S(2)}) async-start(s8[7077888]{0:T(1024)(128)(4,1)} %bitcast.11), calls=%async_computation | async-start | bytes 8388608
  499.5 7.5 %slice-start.1 = ((s8[7077888]{0:T(1024)(128)(4,1)}), s8[2883584]{0:T(1024)(128)(4,1)S(1)}, s32[]{:S(2)}) async-start(s8[7077888]{0:T(1024)(128)(4,1)} %bitcast.11), calls=%async_computation.1 | async-start | bytes 5767168
  509.5 5.1 copy-start.2
  509.5 5.9 %copy-start.1 = (bf16[256,1536]{1,0:T(8,128)(2,1)S(1)}, bf16[256,1536]{1,0:T(8,128)(2,1)}, u32[]{:S(2)}) copy-start(bf16[256,1536]{1,0:T(8,128)(2,1)} %get-tuple-element.52) | copy-start | bytes 2359300

commit v4 on v3

--- a/solution.py
+++ b/solution.py
@@ -425,11 +425,11 @@
 
         lax.fori_loop(0, heads * (rows // TILE), tile, 0)
 
-    ticks = [[functools.partial(shared_wo.spread, 0), functools.partial(shared_w.spread, 0)],
-             [functools.partial(shared_w.spread, 1), functools.partial(shared_wo.forward, 0),
-              functools.partial(cots.hand_on, 2)],
-             [functools.partial(shared_w.forward, 0)] + [functools.partial(cots.hand_on, d) for d in range(3, blocks)],
-             [functools.partial(shared_w.forward, 1)]]
+    ticks = [[functools.partial(cots.hand_on, 2), functools.partial(shared_wo.spread, 0),
+              functools.partial(shared_w.spread, 0)],
+             [functools.partial(shared_w.spread, 1), functools.partial(shared_wo.forward, 0)],
+             [functools.partial(shared_w.forward, 0)],
+             [functools.partial(shared_w.forward, 1)] + [functools.partial(cots.hand_on, d) for d in range(3, blocks)]]
 
     def tick():
         if ticks:
@@ -444,7 +444,8 @@
         lanes.put(kvc + b, kv_half(b, at.c), kv_half(b, at.c), when=there, head=at.sib)
         lanes.arrived(kvc + b, kv_half(b, 1 - at.c), when=there, head=at.sib)
         pl.when(there)(functools.partial(block, b))
-        tick()
+        if d < blocks - 1:
+            tick()
 
     for hh in range(heads):
         total = l_ref[hh]
@@ -704,10 +705,12 @@
     else:
         for load in cot_loads:
             load.wait()
-    for k in (2, 3):
-        late.forward(k)
-    for k in (2, 3):
-        late.finish(k)
+    def second_expert():
+        for k in (2, 3):
+            late.forward(k)
+        for k in (2, 3):
+            late.finish(k)
+
     back = ColumnSum(at, lanes, dx_ref, land_ref)
     lane = lax.broadcasted_iota(jnp.int32, (own_rows, LANES), 1)
     tile = 256
@@ -715,7 +718,7 @@
     def y_copy(b):
         return pltpu.make_async_copy(y_ref, y_out.at[b], y_sem)
 
-    def block(b, first):
+    def block(b, first, between=None):
         if big:
             move(xb_ref.at[b], xb_stage)
             move(cot_hbm.at[b], cot_ref)
@@ -756,7 +759,13 @@
                 acc_ref[:, y * half:(y + 1) * half] += mm(dgu_ref[e, band_all, :], w_ref[e, y, :, :width], NT)
             return 0
 
-        lax.fori_loop(0, experts, hidden, 0)
+        if between is None:
+            lax.fori_loop(0, experts, hidden, 0)
+        else:
+            hidden(0, 0)
+            between()
+            for e in range(1, experts):
+                hidden(e, 0)
         part = dx_stage if big else dx_ref.at[b]
         part[:, :width] = acc_ref[...].astype(BF16)
         part[:, width:] = split_lanes(gg_ref[...])
@@ -790,7 +799,8 @@
         else:
             xt_ref[:, lanes_all] = x_in[:, :width].astype(F32).T.astype(BF16)
 
-        pl.when(jnp.logical_not(first))(lambda: y_copy(b).wait())
+        if not first:
+            y_copy(b).wait()
         for y in range(2):
             total = mm(ga_ref[0], w_ref[0, y, :, width:])
             for e in range(1, experts):
@@ -800,7 +810,7 @@
 
     def distance(d, _):
         for b, origin, to in ((me - d, me - 1, me + 1), (me + d, me + 1, me - 1)):
-            @pl.when((d > 0) & (b >= 0) & (b < blocks))
+            @pl.when((b >= 0) & (b < blocks))
             def _(b=b, origin=origin, to=to):
                 xs_copy(b, origin, 0).wait_recv()
                 pl.when((to >= 0) & (to < blocks))(lambda: xs_copy(b, to, b).start())
@@ -808,15 +818,16 @@
         def side(s, _):
             b = jnp.where(s == 0, me - d, me + d)
 
-            @pl.when((b >= 0) & (b < blocks) & ((d > 0) | (s == 0)))
+            @pl.when((b >= 0) & (b < blocks))
             def _():
-                block(jnp.clip(b, 0, blocks - 1), d == 0)
+                block(jnp.clip(b, 0, blocks - 1), False)
 
             return 0
 
         return lax.fori_loop(0, 2, side, 0)
 
-    lax.fori_loop(0, blocks, distance, 0)
+    block(me, True, second_expert)
+    lax.fori_loop(1, blocks, distance, 0)
     y_copy(me).wait()
 
     def add(b, rows):
@@ -987,7 +998,6 @@
         self.rows = grads.shape[1] // self.CHUNKS
         n = self.CHUNKS
         self.ys, self.xr, self.cg = [lanes.slots(n) for _ in range(3)]
-        self.sent = []
         self.kept = []
 
     def chunk(self, k):
@@ -999,16 +1009,12 @@
         for copy in self.loads:
             copy.start()
 
-    def to_y(self):
-        self.loads[0].wait()
-        for k in range(self.CHUNKS):
+    def to_y(self, first, last):
+        if first == 0:
+            self.loads[0].wait()
+        for k in range(first, last):
             rows = self.chunk(k)
-            self.sent.append(self.lanes.put(
-                self.ys + k, self.own.at[self.at.oy, rows, :], self.land_y.at[rows, :], fsdp=self.at.oy))
-
-    def y_sent(self):
-        for copy in self.sent:
-            self.lanes.settle(copy)
+            self.lanes.put(self.ys + k, self.own.at[self.at.oy, rows, :], self.land_y.at[rows, :], fsdp=self.at.oy)
 
     def to_x(self, k):
         at, rows = self.at, self.chunk(k)
@@ -1140,7 +1146,7 @@
     output = OutputSums(at, lanes, dwo_ref, dwo_y, dwo_z, dwo_land)
     sums = ColumnSum(at, lanes, yp_ref, y_land)
     experts.load()
-    forward, near, far, _ = gather_heads(at, lanes, attn_ref, ag_ref)
+    forward, near, far, passed = gather_heads(at, lanes, attn_ref, ag_ref)
 
     def load(src, dst, sem):
         copy = pltpu.make_async_copy(src, dst, load_sem.at[sem])
@@ -1154,7 +1160,7 @@
     y_load = load(y_in, yp_ref, 3)
     if not big:
         kv_load = load(kv_in, kv_ref, 4)
-    experts.to_y()
+    experts.to_y(0, 6)
     y_load.wait()
     for b in range(blocks):
         sums.first_send(b)
@@ -1336,7 +1342,7 @@
                       dw_y.at[pl.ds(p * part, part), cols_out], fsdp=at.oy)
 
     weight_to_y(0, query_cols)
-    experts.to_x(6)
+    experts.share(3)
 
     @pl.when(at.c == 0)
     def _():
@@ -1356,14 +1362,15 @@
 
     dpre_ref[:, qcols:] = jnp.where(at.c == 0, unrotate(dkv_ref[...]), dkv_ref[...]).astype(BF16)
     weight_to_y(1, keyval_cols)
+    experts.to_y(6, 8)
 
     def input_part(head):
         return mm(dpre_ref[aligned(head * own_rows, own_rows), :], w_ref[...], NT)
 
-    experts.y_sent()
+    lanes.settle(passed[0])
 
     def dn_ref(i):
-        return own_ref.at[at.oy, i * own_rows:(i + 1) * own_rows, :width]
+        return ag_ref.at[i * own_rows:(i + 1) * own_rows, :]
 
     relay, direct, across = lanes.slots(), lanes.slots(), lanes.slots()
     dn_ref(0)[...] = input_part(at.xs).astype(BF16)
@@ -1373,8 +1380,6 @@
     lanes.arrived(relay, dn_sib.at[0], head=at.sib)
     dn_ref(1)[...] = (input_part(at.xn) + dn_sib[0].astype(F32)).astype(BF16)
     lanes.put(across, dn_ref(1), dn_x, head=at.xn)
-    experts.to_x(7)
-    experts.share(3)
     experts.share(4)
     weight_half(at.y, slice(None))
     output.to_y(fetch(dwo_stage))
@@ -1387,8 +1392,9 @@
         total = dw_ref[rows_p, :].astype(F32) + dw_y[pl.ds(p * part, part), :].astype(F32)
         dw_ref[rows_p, :] = total.astype(BF16)
         lanes.put(zr + at.z, dw_ref.at[rows_p, :], dw_z.at[at.z], when=at.z != p, blk=p)
+    output.share()
+    experts.to_x(6)
     experts.share(5)
-    output.share()
 
     move(res_hbm, acc_ref)
     if big:
@@ -1420,6 +1426,7 @@
     sm_ref[gain_row:gain_row + 1, :] = jnp.sum(own * hat, axis=0, keepdims=True)
     sa, sb, sy, sz = lanes.slots(), lanes.slots(), lanes.slots(), lanes.slots(blocks)
     lanes.put(sa, sm_ref, sm_a, head=at.sib)
+    experts.to_x(7)
     experts.share(6)
 
     p = at.z % parts

time: 524 us -> 524 us (level)
    pallas_call x1, Pallas kernels: 152 us -> 146 us  [expert_layer(): pl.pallas_call(expert_kernel, out_shape=(sds((own_rows, width), F32), sds...]
where the time goes in v4:
time: 524 us; the launch traced here: 517 us
  Pallas kernels  481 us (92%)
  other arithmetic  28.6 us (5%)
  local copies, waits for them, and re-layouts  6 us (1%)
    pallas_call x1, Pallas kernels, backward(): pl.pallas_call(back_kernel, out_shape=(sds((own_rows, width), BF16), sds(...  224 us
    pallas_call x1, Pallas kernels, expert_layer(): pl.pallas_call(expert_kernel, out_shape=(sds((own_rows, width), F32), sds...  146 us
    pallas_call x1, Pallas kernels, front(): pl.pallas_call(front_kernel, out_shape=(sds((heads, rows, HEAD), BF16), s...  111 us

profile of v4, /device:TPU:27, one launch (start us, length us, event | category | flops | bytes accessed | tf_op | source)
XLA Modules:
  0.0 516.9 jit_solution(3674552905520111378)
XLA Ops:
  0.7 0.1 pad.7.clone
  0.7 1.4 fusion.2
  2.2 3.2 fusion.6.start_ref
  5.4 0.7 broadcast_in_dim.33
  6.1 0.7 broadcast_in_dim.34
  6.8 1.4 maximum_maximum_fusion.small_ref
  8.2 0.9 fusion
  9.1 0.7 convert_element_type.49.chosen_ref
  9.8 1.9 fusion.1
  11.7 1.3 pad_maximum_fusion
  13.0 111.4 %shard_map.195 = (bf16[3,1024,128]{2,1,0:T(8,128)(2,1)}, bf16[1024,384]{1,0:T(8,128)(2,1)}, bf16[384,1024]{1,0:T(8,128)(2,1)}, f32[3,1,1024]{2,1,0:T(1,128)}, bf...) custom-call(bf16[256,1536]{1,0:T(8,128)(2,1)} %bitcast.8, ...), custom_call_target="tpu_custom_call" | custom-call | tf_op jit(solution)/shard_map/pallas_call | solution.py:488
  124.4 146.1 %shard_map.196 = (f32[256,1536]{1,0:T(8,128)}, f32[256,1536]{1,0:T(8,128)}, bf16[256,1536]{1,0:T(8,128)(2,1)}, f32[16,1536]{1,0:T(8,128)}, bf16[2,768,2304]{2,1,...) custom-call(bf16[1024,384]{1,0:T(8,128)(2,1)} %get-tuple-element.34.o_ref, ...), custom_call_target="tpu_custom_call" | custom-call | tf_op jit(solution)/shard_map/pallas_call | solution.py:953
  270.5 223.7 %shard_map.197 = (bf16[256,1536]{1,0:T(8,128)(2,1)}, bf16[256,1536]{1,0:T(8,128)(2,1)}, f32[16,768]{1,0:T(8,128)}, bf16[768,512]{1,0:T(8,128)(2,1)}, bf16[2,768,...) custom-call(bf16[256,1536]{1,0:T(8,128)(2,1)} %get-tuple-element.39.a, ...), custom_call_target="tpu_custom_call" | custom-call | tf_op jit(solution)/shard_map/pallas_call | solution.py:1523
  494.2 1.4 slice_reduce_fusion
  495.6 1.3 slice_bitcast_fusion
  496.9 2.6 convert_element_type.51
  499.6 4.6 convert_element_type.50
  504.2 2.8 convert_element_type.52
  507.1 0.0 slice-done
  507.1 2.5 slice_convert_fusion.1
  509.6 5.1 slice_convert_fusion
  514.7 0.9 copy.25
  515.6 0.0 copy-done.1
  515.6 0.9 copy.26
  (12 shorter events, 0.0 us)
Async XLA Ops:
  496.9 7.3 %copy-start = (bf16[768,1536]{1,0:T(8,128)(2,1)S(1)}, bf16[768,1536]{1,0:T(8,128)(2,1)}, u32[]{:S(2)}) copy-start(bf16[768,1536]{1,0:T(8,128)(2,1)} %get-tuple-element.56) | copy-start | bytes 7077892
  496.9 10.1 %slice-start = ((s8[7077888]{0:T(1024)(128)(4,1)}), s8[4194304]{0:T(1024)(128)(4,1)S(1)}, s32[]{:S(2)}) async-start(s8[7077888]{0:T(1024)(128)(4,1)} %bitcast.11), calls=%async_computation | async-start | bytes 8388608
  499.6 7.5 %slice-start.1 = ((s8[7077888]{0:T(1024)(128)(4,1)}), s8[2883584]{0:T(1024)(128)(4,1)S(1)}, s32[]{:S(2)}) async-start(s8[7077888]{0:T(1024)(128)(4,1)} %bitcast.11), calls=%async_computation.1 | async-start | bytes 5767168
  509.6 5.1 copy-start.2
  509.6 5.9 %copy-start.1 = (bf16[256,1536]{1,0:T(8,128)(2,1)S(1)}, bf16[256,1536]{1,0:T(8,128)(2,1)}, u32[]{:S(2)}) copy-start(bf16[256,1536]{1,0:T(8,128)(2,1)} %get-tuple-element.52) | copy-start | bytes 2359300

commit v5 on v4

--- a/solution.py
+++ b/solution.py
@@ -264,7 +264,8 @@
 
 
 def front_kernel(x_ref, small_ref, wq_hbm, wkv_hbm, wo_hbm, win_hbm, wout_hbm, cot_hbm, cos_ref, sin_ref, start_ref,
-                 q_ref, o_ref, ot_ref, lse_ref, n1_ref, small_out, wqkv_out, kv_out, wo_out, w_out, cot_out,
+                 o_ref, ot_ref, lse_ref, small_out, q_out, n1_out, wqkv_out, kv_out, wo_out, w_out, cot_out,
+                 q_ref, n1_ref,
                  xg_ref, small_land, wqkv_ref, kv_ref, m_ref, l_ref, acc_ref, vt_ref, wo_ref, w_ref, cot_ref,
                  load_sem, send_sem, recv_sem):
     heads, rows, _ = q_ref.shape
@@ -392,7 +393,7 @@
         return kv_ref.at[b, core]
 
     lanes.put(kvs + me, kv_half(me, at.c), kv_half(me, at.c), when=me < blocks - 1, blk=me + 1)
-    late = [copy_here(wqkv_ref, wqkv_out), copy_here(wo_ref.at[own_half, :], wo_out.at[own_half, :]),
+    late = [copy_here(q_ref, q_out), copy_here(n1_ref, n1_out), copy_here(wqkv_ref, wqkv_out), copy_here(wo_ref.at[own_half, :], wo_out.at[own_half, :]),
             copy_here(w_ref.at[:, at.y], w_out.at[:, at.y])]
 
     m_ref[...] = jnp.full_like(m_ref, MASKED)
@@ -453,12 +454,9 @@
         ot_ref[hh * HEAD:(hh + 1) * HEAD, :] = done.astype(BF16)
         o_ref[:, hh * HEAD:(hh + 1) * HEAD] = done.T.astype(BF16)
         lse_ref[hh] = m_ref[hh] + jnp.log2(total)
-    kv_copies = [pltpu.make_async_copy(kv_ref.at[b], kv_out.at[b], load_sem.at[15]) for b in range(blocks)]
+    kv_copies = [pltpu.make_async_copy(kv_ref.at[b], kv_out.at[b], load_sem.at[16 + b]) for b in range(blocks)]
     for b, copy in enumerate(kv_copies):
-        @pl.when(b <= me)
-        def _(copy=copy):
-            copy.start()
-            copy.wait()
+        pl.when(b <= me)(copy.start)
     while ticks:
         tick()
     shared_wo.finish(0)
@@ -472,6 +470,8 @@
     late.append(copy_here(w_ref.at[:, at.oy], w_out.at[:, at.oy]))
     for copy in late:
         copy.wait()
+    for b, copy in enumerate(kv_copies):
+        pl.when(b <= me)(copy.wait)
     lanes.drain()
 
 
@@ -488,12 +488,12 @@
     return pl.pallas_call(
         front_kernel,
         out_shape=(
-            sds((heads, rows, HEAD), BF16),
             sds((rows, qcols), BF16),
             sds((qcols, rows), BF16),
             sds((heads, 1, rows), F32),
+            sds((small.shape[0], width), BF16),
+            sds((heads, rows, HEAD), BF16),
             sds((rows, width), BF16),
-            sds((small.shape[0], width), BF16),
             sds((width, qcols + 2 * HEAD), BF16),
             sds((blocks, 2, rows, HEAD), BF16),
             sds((width, width), BF16),
@@ -501,8 +501,10 @@
             sds((blocks, own_rows, width), BF16),
         ),
         in_specs=[vm, vm] + [hbm] * 6 + [vm] * 3,
-        out_specs=[vm] * 6 + [hbm] * 5,
+        out_specs=[vm] * 4 + [hbm] * 7,
         scratch_shapes=[
+            pltpu.VMEM((heads, rows, HEAD), BF16),
+            pltpu.VMEM((rows, width), BF16),
             pltpu.VMEM((rows, width), BF16),
             pltpu.VMEM(small.shape, BF16),
             pltpu.VMEM((width, qcols + 2 * HEAD), BF16),
@@ -514,7 +516,7 @@
             pltpu.VMEM((width, width), BF16),
             pltpu.VMEM((2, 2, half, width + half), BF16),
             pltpu.VMEM((blocks, own_rows, width), BF16),
-            pltpu.SemaphoreType.DMA((16,)),
+            pltpu.SemaphoreType.DMA((16 + blocks,)),
         ] + semaphores(blocks),
         compiler_params=pltpu.CompilerParams(
             vmem_limit_bytes=VMEM_BYTES, collective_id=0, has_side_effects=True),
@@ -1307,6 +1309,7 @@
     closing(me, kv_own)
     to_sibling(me, None)
     experts.to_x(5)
+    output.to_y(fetch(dwo_stage))
     for d in range(1, blocks):
         sums.relay(1, d, add)
 
@@ -1363,6 +1366,7 @@
     dpre_ref[:, qcols:] = jnp.where(at.c == 0, unrotate(dkv_ref[...]), dkv_ref[...]).astype(BF16)
     weight_to_y(1, keyval_cols)
     experts.to_y(6, 8)
+    output.share()
 
     def input_part(head):
         return mm(dpre_ref[aligned(head * own_rows, own_rows), :], w_ref[...], NT)
@@ -1382,7 +1386,7 @@
     lanes.put(across, dn_ref(1), dn_x, head=at.xn)
     experts.share(4)
     weight_half(at.y, slice(None))
-    output.to_y(fetch(dwo_stage))
+    output.take_over()
 
     zr = lanes.slots(blocks)
     for p in range(parts):
@@ -1392,7 +1396,6 @@
         total = dw_ref[rows_p, :].astype(F32) + dw_y[pl.ds(p * part, part), :].astype(F32)
         dw_ref[rows_p, :] = total.astype(BF16)
         lanes.put(zr + at.z, dw_ref.at[rows_p, :], dw_z.at[at.z], when=at.z != p, blk=p)
-    output.share()
     experts.to_x(6)
     experts.share(5)
 
@@ -1455,7 +1458,6 @@
     lanes.arrived(sa, sm_a, head=at.sib)
     sm_a[...] = sm_a[...] + sm_ref[...]
     lanes.put(sb, sm_a, sm_b, head=at.xn)
-    output.take_over()
     experts.share(7)
 
     lanes.arrived(sb, sm_b, head=at.xn)
@@ -1597,7 +1599,7 @@
     start = sum(jnp.where(doc_q > d, jnp.sum((doc == d).astype(jnp.int32)), 0) for d in range(DOCUMENTS - 1))[None, :]
     chosen = jnp.any(routes[0][:, :, None] == jnp.arange(LANES, dtype=jnp.int32), axis=1).astype(F32)
 
-    q, mixed, mixed_t, lse, n1, small, wqkv, kv_all, wo, w_experts, cots = front(
+    mixed, mixed_t, lse, small, q, n1, wqkv, kv_all, wo, w_experts, cots = front(
         blocks, tokens[0], small, query_weight, keyvalue_weight, output_weight, expert_in, expert_out,
         cotangent[0], cosine, sine, start)
     res1, res_grad, attn_grad, d_small, grads, y_parts = expert_layer(

time: 524 us -> 520 us (level)
  the two profiles are of different devices: /device:TPU:27 before, /device:TPU:9 now
where the time goes in v5:
time: 520 us; the launch traced here: 513 us
  Pallas kernels  477 us (92%)
  other arithmetic  28.6 us (6%)
  local copies, waits for them, and re-layouts  6 us (1%)
    pallas_call x1, Pallas kernels, backward(): pl.pallas_call(back_kernel, out_shape=(sds((own_rows, width), BF16), sds(...  224 us
    pallas_call x1, Pallas kernels, expert_layer(): pl.pallas_call(expert_kernel, out_shape=(sds((own_rows, width), F32), sds...  161 us
    pallas_call x1, Pallas kernels, front(): pl.pallas_call(front_kernel, out_shape=(sds((rows, qcols), BF16), sds((qc...  91.5 us

profile of v5, /device:TPU:9, one launch (start us, length us, event | category | flops | bytes accessed | tf_op | source)
XLA Modules:
  0.0 512.7 jit_solution(3851540815310996594)
XLA Ops:
  0.7 0.1 pad.7.clone
  0.7 1.4 fusion.2
  2.2 3.2 fusion.6.start_ref
  5.4 0.7 broadcast_in_dim.33
  6.1 0.7 broadcast_in_dim.34
  6.8 1.4 maximum_maximum_fusion.small_ref
  8.2 0.9 fusion
  9.1 0.7 convert_element_type.49.chosen_ref
  9.8 1.9 fusion.1
  11.7 1.3 pad_maximum_fusion
  13.0 91.5 %shard_map.195 = (bf16[1024,384]{1,0:T(8,128)(2,1)}, bf16[384,1024]{1,0:T(8,128)(2,1)}, f32[3,1,1024]{2,1,0:T(1,128)}, bf16[16,1536]{1,0:T(8,128)(2,1)}, bf16[3,...) custom-call(bf16[256,1536]{1,0:T(8,128)(2,1)} %bitcast.8, ...), custom_call_target="tpu_custom_call" | custom-call | tf_op jit(solution)/shard_map/pallas_call | solution.py:488
  104.4 161.0 %shard_map.196 = (f32[256,1536]{1,0:T(8,128)}, f32[256,1536]{1,0:T(8,128)}, bf16[256,1536]{1,0:T(8,128)(2,1)}, f32[16,1536]{1,0:T(8,128)}, bf16[2,768,2304]{2,1,...) custom-call(bf16[1024,384]{1,0:T(8,128)(2,1)} %get-tuple-element.34.o_ref, ...), custom_call_target="tpu_custom_call" | custom-call | tf_op jit(solution)/shard_map/pallas_call | solution.py:955
  265.4 224.5 %shard_map.197 = (bf16[256,1536]{1,0:T(8,128)(2,1)}, bf16[256,1536]{1,0:T(8,128)(2,1)}, f32[16,768]{1,0:T(8,128)}, bf16[768,512]{1,0:T(8,128)(2,1)}, bf16[2,768,...) custom-call(bf16[256,1536]{1,0:T(8,128)(2,1)} %get-tuple-element.39.a, ...), custom_call_target="tpu_custom_call" | custom-call | tf_op jit(solution)/shard_map/pallas_call | solution.py:1525
  489.9 1.4 slice_reduce_fusion
  491.4 1.3 slice_bitcast_fusion
  492.7 2.6 convert_element_type.51
  495.4 4.6 convert_element_type.50
  500.0 0.0 copy-done
  500.0 2.8 convert_element_type.52
  502.8 0.0 slice-done.1
  502.8 2.5 slice_convert_fusion.1
  505.4 5.1 slice_convert_fusion
  510.5 0.9 copy.25
  511.3 0.9 copy.26
  (12 shorter events, 0.0 us)
Async XLA Ops:
  492.7 7.3 %copy-start = (bf16[768,1536]{1,0:T(8,128)(2,1)S(1)}, bf16[768,1536]{1,0:T(8,128)(2,1)}, u32[]{:S(2)}) copy-start(bf16[768,1536]{1,0:T(8,128)(2,1)} %get-tuple-element.56) | copy-start | bytes 7077892
  492.7 10.1 %slice-start = ((s8[7077888]{0:T(1024)(128)(4,1)}), s8[4194304]{0:T(1024)(128)(4,1)S(1)}, s32[]{:S(2)}) async-start(s8[7077888]{0:T(1024)(128)(4,1)} %bitcast.11), calls=%async_computation | async-start | bytes 8388608
  495.4 7.5 %slice-start.1 = ((s8[7077888]{0:T(1024)(128)(4,1)}), s8[2883584]{0:T(1024)(128)(4,1)S(1)}, s32[]{:S(2)}) async-start(s8[7077888]{0:T(1024)(128)(4,1)} %bitcast.11), calls=%async_computation.1 | async-start | bytes 5767168
  505.4 5.1 copy-start.2
  505.4 5.9 %copy-start.1 = (bf16[256,1536]{1,0:T(8,128)(2,1)S(1)}, bf16[256,1536]{1,0:T(8,128)(2,1)}, u32[]{:S(2)}) copy-start(bf16[256,1536]{1,0:T(8,128)(2,1)} %get-tuple-element.52) | copy-start | bytes 2359300

commit v6 on v5

--- a/solution.py
+++ b/solution.py
@@ -1309,7 +1309,6 @@
     closing(me, kv_own)
     to_sibling(me, None)
     experts.to_x(5)
-    output.to_y(fetch(dwo_stage))
     for d in range(1, blocks):
         sums.relay(1, d, add)
 
@@ -1366,7 +1365,6 @@
     dpre_ref[:, qcols:] = jnp.where(at.c == 0, unrotate(dkv_ref[...]), dkv_ref[...]).astype(BF16)
     weight_to_y(1, keyval_cols)
     experts.to_y(6, 8)
-    output.share()
 
     def input_part(head):
         return mm(dpre_ref[aligned(head * own_rows, own_rows), :], w_ref[...], NT)
@@ -1386,7 +1384,7 @@
     lanes.put(across, dn_ref(1), dn_x, head=at.xn)
     experts.share(4)
     weight_half(at.y, slice(None))
-    output.take_over()
+    output.to_y(fetch(dwo_stage))
 
     zr = lanes.slots(blocks)
     for p in range(parts):
@@ -1396,6 +1394,7 @@
         total = dw_ref[rows_p, :].astype(F32) + dw_y[pl.ds(p * part, part), :].astype(F32)
         dw_ref[rows_p, :] = total.astype(BF16)
         lanes.put(zr + at.z, dw_ref.at[rows_p, :], dw_z.at[at.z], when=at.z != p, blk=p)
+    output.share()
     experts.to_x(6)
     experts.share(5)
 
@@ -1458,6 +1457,7 @@
     lanes.arrived(sa, sm_a, head=at.sib)
     sm_a[...] = sm_a[...] + sm_ref[...]
     lanes.put(sb, sm_a, sm_b, head=at.xn)
+    output.take_over()
     experts.share(7)
 
     lanes.arrived(sb, sm_b, head=at.xn)

time: 520 us -> 520 us (level)
  the two profiles are of different devices: /device:TPU:9 before, /device:TPU:27 now
where the time goes in v6:
time: 520 us; the launch traced here: 513 us
  Pallas kernels  477 us (92%)
  other arithmetic  28.6 us (6%)
  local copies, waits for them, and re-layouts  6 us (1%)
    pallas_call x1, Pallas kernels, backward(): pl.pallas_call(back_kernel, out_shape=(sds((own_rows, width), BF16), sds(...  224 us
    pallas_call x1, Pallas kernels, expert_layer(): pl.pallas_call(expert_kernel, out_shape=(sds((own_rows, width), F32), sds...  146 us
    pallas_call x1, Pallas kernels, front(): pl.pallas_call(front_kernel, out_shape=(sds((rows, qcols), BF16), sds((qc...  107 us

profile of v6, /device:TPU:27, one launch (start us, length us, event | category | flops | bytes accessed | tf_op | source)
XLA Modules:
  0.0 513.0 jit_solution(7037678791752741114)
XLA Ops:
  0.7 0.1 pad.7.clone
  0.7 1.4 fusion.2
  2.2 3.2 fusion.6.start_ref
  5.4 0.7 broadcast_in_dim.33
  6.1 0.7 broadcast_in_dim.34
  6.8 1.4 maximum_maximum_fusion.small_ref
  8.2 0.9 fusion
  9.1 0.7 convert_element_type.49.chosen_ref
  9.8 1.9 fusion.1
  11.7 1.3 pad_maximum_fusion
  13.0 107.3 %shard_map.195 = (bf16[1024,384]{1,0:T(8,128)(2,1)}, bf16[384,1024]{1,0:T(8,128)(2,1)}, f32[3,1,1024]{2,1,0:T(1,128)}, bf16[16,1536]{1,0:T(8,128)(2,1)}, bf16[3,...) custom-call(bf16[256,1536]{1,0:T(8,128)(2,1)} %bitcast.8, ...), custom_call_target="tpu_custom_call" | custom-call | tf_op jit(solution)/shard_map/pallas_call | solution.py:488
  120.3 146.3 %shard_map.196 = (f32[256,1536]{1,0:T(8,128)}, f32[256,1536]{1,0:T(8,128)}, bf16[256,1536]{1,0:T(8,128)(2,1)}, f32[16,1536]{1,0:T(8,128)}, bf16[2,768,2304]{2,1,...) custom-call(bf16[1024,384]{1,0:T(8,128)(2,1)} %get-tuple-element.34.o_ref, ...), custom_call_target="tpu_custom_call" | custom-call | tf_op jit(solution)/shard_map/pallas_call | solution.py:955
  266.6 223.7 %shard_map.197 = (bf16[256,1536]{1,0:T(8,128)(2,1)}, bf16[256,1536]{1,0:T(8,128)(2,1)}, f32[16,768]{1,0:T(8,128)}, bf16[768,512]{1,0:T(8,128)(2,1)}, bf16[2,768,...) custom-call(bf16[256,1536]{1,0:T(8,128)(2,1)} %get-tuple-element.39.a, ...), custom_call_target="tpu_custom_call" | custom-call | tf_op jit(solution)/shard_map/pallas_call | solution.py:1525
  490.3 1.4 slice_reduce_fusion
  491.7 1.3 slice_bitcast_fusion
  493.1 2.6 convert_element_type.51
  495.7 4.6 convert_element_type.50
  500.4 2.8 convert_element_type.52
  503.2 0.0 slice-done
  503.2 2.5 slice_convert_fusion.1
  505.8 5.1 slice_convert_fusion
  510.8 0.9 copy.25
  511.7 0.0 copy-done.1
  511.7 0.9 copy.26
  (12 shorter events, 0.0 us)
Async XLA Ops:
  493.1 7.3 %copy-start = (bf16[768,1536]{1,0:T(8,128)(2,1)S(1)}, bf16[768,1536]{1,0:T(8,128)(2,1)}, u32[]{:S(2)}) copy-start(bf16[768,1536]{1,0:T(8,128)(2,1)} %get-tuple-element.56) | copy-start | bytes 7077892
  493.1 10.1 %slice-start = ((s8[7077888]{0:T(1024)(128)(4,1)}), s8[4194304]{0:T(1024)(128)(4,1)S(1)}, s32[]{:S(2)}) async-start(s8[7077888]{0:T(1024)(128)(4,1)} %bitcast.11), calls=%async_computation | async-start | bytes 8388608
  495.7 7.5 %slice-start.1 = ((s8[7077888]{0:T(1024)(128)(4,1)}), s8[2883584]{0:T(1024)(128)(4,1)S(1)}, s32[]{:S(2)}) async-start(s8[7077888]{0:T(1024)(128)(4,1)} %bitcast.11), calls=%async_computation.1 | async-start | bytes 5767168
  505.8 5.1 copy-start.2
  505.8 5.9 %copy-start.1 = (bf16[256,1536]{1,0:T(8,128)(2,1)S(1)}, bf16[256,1536]{1,0:T(8,128)(2,1)}, u32[]{:S(2)}) copy-start(bf16[256,1536]{1,0:T(8,128)(2,1)} %get-tuple-element.52) | copy-start | bytes 2359300
